TPU v7x, 32 devices: a whole 2x2x4 slice. The times are simulated.
32 devices in a mesh: groups: 2 (over y), dp: 16 (over z, x, core).
Axes of the slice: x: 2, y: 2, z: 4, core: 2. Of those that a mesh axis runs over, the one named last changes fastest.
Arguments:
- tokens: bfloat16 [256, 8192], P(('groups', 'dp')), parts along dimension 0, may hold values from -6 to 6
- token_adapter_index: int32 [256, 1], P(('groups', 'dp')), parts along dimension 0, may hold values from 0 to 15; in each aligned block of 128 rows (0 to 127, 128 to 255, ...) at most 32 rows name the same one
- adapter_slot_index: int32 [16], replicated, may hold values from 0 to 15, each once
- gate_matrix: bfloat16 [8192, 28672], P(None, 'dp'), may hold values from -0.0625 to 0.0625
- up_matrix: bfloat16 [8192, 28672], P(None, 'dp'), may hold values from -0.0625 to 0.0625
- adapter_down_factor: bfloat16 [16, 8192, 64], P('dp'), may hold values from -0.0625 to 0.0625
- adapter_up_factor: bfloat16 [16, 64, 28672], P('dp'), may hold values from -0.75 to 0.75
Outputs:
- hidden: bfloat16 [256, 28672], P('groups', 'dp'), parts along dimension 0
There are 2 independent parts, one for each index of `groups`. A program takes and returns all parts, laid end to end along the dimension named above; an argument that names none is the same for every part. Nothing has to cross between parts.
Inputs may be any that keep to these rules, and one draw needn't show every extreme that they name: `token_adapter_index`: no adapter is named by more than 32 rows of a group, and one is named by exactly 32. `adapter_slot_index`: each slot holds exactly one adapter.
All inputs are finite; a program needn't handle non-finite values.
Results may differ from a plain program's by a relative error of at most 0.0075.
Values may be sent and summed in bfloat16 or wider, within the bound.
No kernel may reach another device: no remote copies, remote signals or barrier semaphores. Data moves between devices by JAX's collectives and lax.ppermute only.
A program may use at most 192 MiB of HBM per device.

v0:
```python
import functools

import jax
import jax.numpy as jnp
from jax import lax
from jax.experimental import pallas as pl
from jax.experimental.pallas import tpu as pltpu
from jax.sharding import PartitionSpec as P

CAP = 32
LANES = 128
PLANES = 4
F32 = jnp.float32
BF16 = jnp.bfloat16


def general_shards(
    tokens,
    token_adapter_index,
    adapter_slot_index,
    gate_matrix,
    up_matrix,
    adapter_down_factor,
    adapter_up_factor,
):
    count = lax.axis_size("dp")
    myself = lax.axis_index("dp")
    all_rows, all_ids = (
        lax.all_gather(tokens, "dp", axis=0, tiled=True),
        lax.all_gather(token_adapter_index, "dp", axis=0, tiled=True),
    )
    total = all_rows.shape[0]
    places = jnp.arange(count, dtype=jnp.int32)
    match = all_ids[:, 0][:, None] == places[None, :]
    slots = jnp.sum(jnp.where(match, adapter_slot_index[None, :], 0), 1)
    slot_match = slots[:, None] == places[None, :]
    onehot = slot_match.astype(jnp.int32)
    ranks = jnp.sum(jnp.cumsum(onehot, 0) * onehot, 1) - 1
    capacity = CAP
    columns = jnp.arange(capacity, dtype=jnp.int32)
    mine = (slots == myself)[:, None] & (ranks[:, None] == columns[None, :])
    row_list = jnp.sum(jnp.where(mine, jnp.arange(total, dtype=jnp.int32)[:, None], 0), 0)
    selected_slot = jnp.take(all_rows, row_list, axis=0)
    reduced_rows = jnp.dot(
        selected_slot, adapter_down_factor[0], preferred_element_type=F32
    ).astype(BF16)
    slot_pieces = lax.all_to_all(adapter_up_factor, "dp", split_axis=2, concat_axis=0, tiled=True)
    all_low = lax.all_gather(reduced_rows, "dp", axis=0, tiled=True)
    rank_width = all_low.shape[1]
    token_low = jnp.take(all_low, slots * capacity + ranks, axis=0)
    expanded = (token_low[:, None, :] * slot_match.astype(BF16)[:, :, None]).reshape(
        total, count * rank_width
    )
    stacked = slot_pieces.reshape(count * rank_width, slot_pieces.shape[2])
    delta = jnp.dot(expanded, stacked, preferred_element_type=F32).astype(BF16)
    gate_base = jnp.dot(all_rows, gate_matrix, preferred_element_type=F32)
    up = jnp.dot(all_rows, up_matrix, preferred_element_type=F32)
    gate = gate_base + delta.astype(F32)
    return (jax.nn.silu(gate) * up).astype(BF16)


ANY = pl.BlockSpec(memory_space=pl.ANY)
HBM = pl.BlockSpec(memory_space=pltpu.HBM)
VMEM = pl.BlockSpec(memory_space=pltpu.VMEM)
ROOMS = (64, 16, 48)
FACTORS = (2, 3)
ROWS = (0, 1)


def cut(u_ref, sems, width, wanted):
    rank = u_ref.shape[0]
    half = rank // 2
    z = lax.axis_index("dp") // 4
    copies = []
    for n, (j, x, c, part, target) in enumerate(wanted):
        at = pl.multiple_of(((lax.bitwise_xor(z, j) * 2 + x) * 2 + c) * width, LANES)
        rows = pl.ds(0, rank) if part is None else pl.ds(pl.multiple_of(part * half, half), half)
        copies.append(pltpu.make_async_copy(u_ref.at[rows, pl.ds(at, width)], target, sems.at[n]))
    for copy in copies:
        copy.start()
    for copy in copies:
        copy.wait()


def position():
    me = lax.axis_index("dp")
    return (me // 2) % 2, me % 2


def cross_kernel(width, u_ref, cross_ref, both_ref, sems):
    (x, c), y = position(), lax.axis_index("groups")
    wanted = []
    for i, j in enumerate(FACTORS):
        place = pl.ds(i * width, width)
        wanted += [(j, 1 - x, c, y, cross_ref.at[:, place]), (j, 1 - x, 1 - c, y, both_ref.at[:, place])]
    cut(u_ref, sems, width, wanted)


def cut_cross(u, width):
    rank = u.shape[0]
    n = 2 * len(FACTORS)
    split = pltpu.VMEM((rank // 2, len(FACTORS) * width), BF16)
    return pl.pallas_call(
        functools.partial(cross_kernel, width),
        out_shape=[split, split],
        in_specs=[HBM],
        out_specs=[VMEM, VMEM],
        scratch_shapes=[pltpu.SemaphoreType.DMA((n,))],
        compiler_params=pltpu.CompilerParams(vmem_limit_bytes=4 * 1024 * 1024),
        cost_estimate=pl.CostEstimate(flops=0, bytes_accessed=2 * rank * n * width, transcendentals=0),
        name="cut_cross",
    )(u)


def repack_kernel(width, u_ref, own_rows_ref, own_ref, core_rows_ref, core_ref, sems):
    x, c = position()
    wanted = []
    for cc, rows_ref, ref in ((1 - c, core_rows_ref, core_ref), (c, own_rows_ref, own_ref)):
        for target, blocks in (
            (ref, [(j, x) for j in FACTORS]),
            (rows_ref, [(j, xx) for xx in (x, 1 - x) for j in ROWS]),
        ):
            for i, (j, xx) in enumerate(blocks):
                wanted.append((j, xx, cc, None, target.at[:, pl.ds(i * width, width)]))
    cut(u_ref, sems, width, wanted)


def repack(u, width):
    rank = u.shape[0]
    n = 2 * (len(FACTORS) + 2 * len(ROWS))
    for_rows = pltpu.VMEM((rank, 2 * len(ROWS) * width), BF16)
    for_factors = pltpu.VMEM((rank, len(FACTORS) * width), BF16)
    return pl.pallas_call(
        functools.partial(repack_kernel, width),
        out_shape=[for_rows, for_factors] * 2,
        in_specs=[HBM],
        out_specs=[VMEM] * 4,
        scratch_shapes=[pltpu.SemaphoreType.DMA((n,))],
        compiler_params=pltpu.CompilerParams(vmem_limit_bytes=4 * 1024 * 1024),
        cost_estimate=pl.CostEstimate(flops=0, bytes_accessed=3 * u.size, transcendentals=0),
        name="repack",
    )(u)


def low_kernel(*refs):
    x_refs, (down_ref, table_ref, distance_ref, distance_column_ref), outs = refs[:4], refs[4:8], refs[8:]
    low_ref, meta_ref, pick_ref, order_ref, rounds_ref = outs
    depth = down_ref.shape[1]
    x = jnp.concatenate([ref[:, :depth] for ref in x_refs], axis=0)
    low = lax.dot_general(x, down_ref[...], (((1,), (1,)), ((), ())), preferred_element_type=F32).astype(BF16)
    ids = jnp.concatenate([ref[:, depth:] for ref in x_refs], axis=0).astype(F32)
    total = ids.shape[0]
    lane = lax.broadcasted_iota(jnp.int32, ids.shape, 1).astype(F32)
    place = lax.broadcasted_iota(jnp.int32, ids.shape, 0).astype(F32)
    table = jnp.broadcast_to(table_ref[...], ids.shape).astype(F32)
    slots = jnp.broadcast_to(jnp.sum(jnp.where(ids == lane, table, 0.0), axis=1, keepdims=True), (total, total))
    slots_row = slots.T
    planes, planes_row = jnp.floor(slots * 0.25), jnp.floor(slots_row * 0.25)
    me = lax.axis_index("dp")
    own_rows = total // lax.axis_size("dp")

    def rows_at(distance, along):
        inner = lax.broadcasted_iota(jnp.int32, ids.shape, along) % own_rows
        owner = lax.bitwise_xor(jnp.broadcast_to(distance, ids.shape), jnp.broadcast_to(me, ids.shape))
        return (owner * own_rows + inner).astype(F32)

    at, at_column = rows_at(distance_ref[...], 1), rows_at(distance_column_ref[...], 0)
    same = planes == planes_row
    ranks_row = jnp.sum(jnp.where(same & (at_column < at), 1.0, 0.0), axis=0, keepdims=True)
    ranks = jnp.sum(jnp.where(same & (at < at_column), 1.0, 0.0), axis=1, keepdims=True)
    mine = jnp.where((slots_row == me.astype(F32)) & (ranks_row == place), 1.0, 0.0).astype(BF16)
    low_ref[...] = jnp.dot(mine, low, preferred_element_type=F32).astype(BF16)
    z = jnp.broadcast_to(me // 4, (1, total))
    meta_ref[0:1, :] = lax.bitwise_xor(planes_row[0:1, :].astype(jnp.int32), z)
    meta_ref[1:2, :] = ranks_row.astype(jnp.int32)
    order_ref[...] = jnp.where(at == place, 1.0, 0.0).astype(BF16)
    room = ROOMS[0]
    wide = lax.broadcasted_iota(jnp.int32, pick_ref.shape, 1)
    block = wide // room
    distance = jnp.where(block < PLANES, block, block - PLANES)
    wanted = lax.bitwise_xor(distance, jnp.broadcast_to(me // 4, distance.shape)).astype(F32)
    found = (planes[:, :1] == wanted) & (ranks == (wide % room).astype(F32))
    pick_ref[...] = jnp.where(found, 1.0, 0.0).astype(BF16)
    most = jnp.max(ranks_row)
    rounds_ref[0] = (most >= room).astype(jnp.int32) + (most >= room + ROOMS[1]).astype(jnp.int32)


def low_rows(x_parts, down, table, distance):
    total = distance.shape[0]
    rank = down.shape[0]
    return pl.pallas_call(
        low_kernel,
        out_shape=[
            jax.ShapeDtypeStruct((total, rank), BF16),
            jax.ShapeDtypeStruct((2, total), jnp.int32),
            jax.ShapeDtypeStruct((total, (PLANES + len(ROWS)) * ROOMS[0]), BF16),
            jax.ShapeDtypeStruct((total, total), BF16),
            jax.ShapeDtypeStruct((1,), jnp.int32),
        ],
        in_specs=[VMEM] * 8,
        out_specs=[VMEM] * 4 + [pl.BlockSpec(memory_space=pltpu.SMEM)],
        compiler_params=pltpu.CompilerParams(vmem_limit_bytes=8 * 1024 * 1024),
        cost_estimate=pl.CostEstimate(flops=0, bytes_accessed=4096, transcendentals=0),
        name="low_rows",
    )(*x_parts, down, table, distance[None, :], distance[:, None])


def delta_kernel(plan, width, e_ref, *refs):
    parts, outs = refs[: len(refs) - len(plan)], refs[len(refs) - len(plan) :]
    e = e_ref[...]
    chip = 2 * parts[0].shape[0]
    if e.shape[1] > chip:
        shape = (e.shape[1] - chip,) * 2
        half = jnp.broadcast_to(lax.axis_index("groups") * (chip // 4), shape)
        here, there = lax.broadcasted_iota(jnp.int32, shape, 0), lax.broadcasted_iota(jnp.int32, shape, 1)
        turn = jnp.where(lax.bitwise_xor(here, half) == there, 1.0, 0.0).astype(BF16)
        beyond = jnp.dot(e[:, chip:], turn, preferred_element_type=F32).astype(BF16)
        e = jnp.concatenate([e[:, :chip], beyond], axis=1)
    for pieces, out in zip(plan, outs):
        stacked = jnp.concatenate(
            [parts[n][at : at + rows, i * width : (i + 1) * width] for n, i, at, rows in pieces], axis=0
        )
        out[...] = jnp.dot(e[:, : stacked.shape[0]], stacked, preferred_element_type=F32).astype(BF16)


def delta_rows(e, parts, plan, width):
    rows = e.shape[0]
    n = len(plan)
    return pl.pallas_call(
        functools.partial(delta_kernel, plan, width),
        out_shape=[jax.ShapeDtypeStruct((rows, width), BF16)] * n,
        in_specs=[VMEM] * (1 + len(parts)),
        out_specs=[VMEM] * n,
        compiler_params=pltpu.CompilerParams(vmem_limit_bytes=8 * 1024 * 1024),
        cost_estimate=pl.CostEstimate(flops=0, bytes_accessed=4096, transcendentals=0),
        name="delta_rows",
    )(e, *parts)


BLOCK = 512
SLOTS = 3
AHEAD = 4


def fetch_kernel(first, after_ref, ref, head_ref, sem):
    copy = pltpu.make_async_copy(ref.at[pl.ds(first, head_ref.shape[0])], head_ref, sem)
    copy.start()
    copy.wait()


def fetch(after, matrix):
    shape = jax.ShapeDtypeStruct((AHEAD * BLOCK, matrix.shape[1]), BF16)
    return pl.pallas_call(
        functools.partial(fetch_kernel, 0),
        out_shape=shape,
        in_specs=[ANY, HBM],
        out_specs=VMEM,
        scratch_shapes=[pltpu.SemaphoreType.DMA],
        compiler_params=pltpu.CompilerParams(vmem_limit_bytes=4 * 1024 * 1024),
        cost_estimate=pl.CostEstimate(flops=0, bytes_accessed=8 * shape.size, transcendentals=0),
        name="fetch",
    )(after, matrix)


def base_kernel(steps, rows, *refs):
    x_refs, (g_ref, u_ref, g_head, u_head), refs = refs[:4], refs[4:8], refs[8:]
    gate_ref, up_ref, x_held, g_held, u_held, x_sems, g_sems, u_sems = refs

    def weights(k, slot):
        at = pl.ds(pl.multiple_of(k * BLOCK, BLOCK), BLOCK)
        return (
            pltpu.make_async_copy(g_ref.at[at], g_held.at[slot], g_sems.at[slot]),
            pltpu.make_async_copy(u_ref.at[at], u_held.at[slot], u_sems.at[slot]),
        )

    columns = pl.ds(0, steps * BLOCK)
    loads = [
        pltpu.make_async_copy(ref.at[:, columns], x_held.at[pl.ds(i * rows, rows)], x_sems.at[i])
        for i, ref in enumerate(x_refs)
    ]
    for copy in loads:
        copy.start()
    for k in range(SLOTS):
        for copy in weights(AHEAD + k, k):
            copy.start()
    for copy in loads:
        copy.wait()
    x = x_held[:, : AHEAD * BLOCK]
    gate_ref[...] = jnp.dot(x, g_head[...], preferred_element_type=F32)
    up_ref[...] = jnp.dot(x, u_head[...], preferred_element_type=F32)

    def step(n, carry):
        slot = lax.rem(n, SLOTS)
        k = n + AHEAD
        gate_copy, up_copy = weights(k, slot)
        x = x_held[:, pl.ds(pl.multiple_of(k * BLOCK, BLOCK), BLOCK)]
        gate_copy.wait()
        gate_ref[...] += jnp.dot(x, g_held[slot], preferred_element_type=F32)
        up_copy.wait()
        up_ref[...] += jnp.dot(x, u_held[slot], preferred_element_type=F32)

        @pl.when(k + SLOTS < steps)
        def _():
            for copy in weights(k + SLOTS, slot):
                copy.start()

        return carry

    lax.fori_loop(0, steps - AHEAD, step, 0)


def base(x_parts, gate_matrix, up_matrix, heads):
    depth, width = gate_matrix.shape
    steps = depth // BLOCK
    rows = x_parts[0].shape[0]
    total = rows * len(x_parts)
    shape = jax.ShapeDtypeStruct((total, width), F32)
    return pl.pallas_call(
        functools.partial(base_kernel, steps, rows),
        out_shape=[shape, shape],
        in_specs=[ANY] * len(x_parts) + [HBM] * 2 + [VMEM] * 2,
        out_specs=[VMEM, VMEM],
        scratch_shapes=[
            pltpu.VMEM((total, depth), BF16),
            pltpu.VMEM((SLOTS, BLOCK, width), BF16),
            pltpu.VMEM((SLOTS, BLOCK, width), BF16),
            pltpu.SemaphoreType.DMA((len(x_parts),)),
            pltpu.SemaphoreType.DMA((SLOTS,)),
            pltpu.SemaphoreType.DMA((SLOTS,)),
        ],
        compiler_params=pltpu.CompilerParams(vmem_limit_bytes=18 * 1024 * 1024),
        cost_estimate=pl.CostEstimate(
            flops=4 * total * depth * width, bytes_accessed=4 * depth * width, transcendentals=0
        ),
        name="base",
    )(*x_parts, gate_matrix, up_matrix, *heads)


def finish_kernel(step, gate_ref, up_ref, pick_ref, order_ref, *refs):
    rows_refs, (out_ref, held, sems) = refs[:-3], refs[-3:]
    writes = []
    for n in range(gate_ref.shape[1] // step):
        at = slice(n * step, (n + 1) * step)
        stacked = jnp.concatenate([ref[:, at] for ref in rows_refs], axis=0)
        gate = gate_ref[:, at] + jnp.dot(pick_ref[...], stacked, preferred_element_type=F32)
        hidden = (gate / (1.0 + jnp.exp(-gate)) * up_ref[:, at]).astype(BF16)
        held[:, at] = jnp.dot(order_ref[...], hidden, preferred_element_type=F32).astype(BF16)
        writes.append(pltpu.make_async_copy(held.at[:, at], out_ref.at[:, at], sems.at[n]))
        writes[-1].start()
    for copy in writes:
        copy.wait()


def finish(gate, up, pick, order, rows_by_plane):
    total, width = gate.shape
    n = 2 if width % (2 * LANES) == 0 else 1
    return pl.pallas_call(
        functools.partial(finish_kernel, width // n),
        out_shape=pltpu.HBM((total, width), BF16),
        in_specs=[VMEM] * (4 + len(rows_by_plane)),
        out_specs=HBM,
        scratch_shapes=[pltpu.VMEM((total, width), BF16), pltpu.SemaphoreType.DMA((n,))],
        compiler_params=pltpu.CompilerParams(vmem_limit_bytes=8 * 1024 * 1024),
        cost_estimate=pl.CostEstimate(flops=0, bytes_accessed=4 * total * width * 4, transcendentals=total * width),
        name="finish",
    )(gate, up, pick, order, *rows_by_plane)


def plane_shards(
    tokens,
    token_adapter_index,
    adapter_slot_index,
    gate_matrix,
    up_matrix,
    adapter_down_factor,
    adapter_up_factor,
):
    count = lax.axis_size("dp")
    me, y = lax.axis_index("dp"), lax.axis_index("groups")
    z = me // 4
    up_factor, gate_matrix, up_matrix = (
        pltpu.with_memory_space_constraint(v, pltpu.HBM) for v in (adapter_up_factor[0], gate_matrix, up_matrix)
    )
    own_rows, depth = tokens.shape
    total = own_rows * count
    width = gate_matrix.shape[1]
    rank = adapter_up_factor.shape[1]

    def swap(value, k):
        return lax.ppermute(value, "dp", [(d, d ^ k) for d in range(count)])

    def other(value):
        return lax.ppermute(value, "groups", [(0, 1), (1, 0)])

    ids = jnp.broadcast_to(token_adapter_index.astype(BF16), (own_rows, LANES))
    packed = jnp.concatenate([tokens, ids], axis=1)
    packed, cross, both = lax.optimization_barrier((packed, *cut_cross(up_factor, width)))
    cross, both = swap(cross, 2), swap(both, 3)
    second, third = swap(packed, 8), swap(packed, 12)
    pair = jnp.concatenate([packed, swap(packed, 2)], axis=0)
    remote = jnp.concatenate([second, third], axis=0)
    own_chip, own_plane, core_chip, core_plane = repack(up_factor, width)
    core_chip, core_plane = swap(core_chip, 1), swap(core_plane, 1)
    gate_head = fetch(own_plane, gate_matrix)
    pair, remote, down, core_chip, core_plane, gate_head = lax.optimization_barrier(
        (pair, remote, adapter_down_factor[0], core_chip, core_plane, gate_head)
    )
    close = jnp.concatenate([pair, swap(pair, 4)], axis=0)
    remote = jnp.concatenate([remote, swap(remote, 2)], axis=0)
    up_head = fetch(pair, up_matrix)
    cross, both, up_head = lax.optimization_barrier((cross, both, up_head))
    crossed = jnp.concatenate([cross, both], axis=0)
    heads = (gate_head, up_head)
    close, remote, heads = lax.optimization_barrier((close, remote, heads))
    x_parts = (close, remote, swap(close, 1), swap(remote, 1))
    distances = [0, 2, 4, 6, 8, 12, 10, 14]
    distances = distances + [k + 1 for k in distances]

    cross_parts = (crossed, other(crossed))
    half = rank // 2

    distance = jnp.array([k for k in distances for _ in range(own_rows)], jnp.int32)
    table = jnp.pad(adapter_slot_index, (0, LANES - count))[None, :]
    low, meta, first, order, rounds = low_rows(x_parts, down.T, table, distance)
    planes, ranks = meta[0], meta[1]

    chip_plan = tuple(((0, i, 0, rank), (1, i, 0, rank)) for i in range(2 * len(ROWS)))
    plane_plan = tuple(
        ((0, i, 0, rank), (1, i, 0, rank)) + tuple((n, i, at, half) for at in (0, half) for n in (2, 3))
        for i in range(len(FACTORS))
    )

    def chip_rows(e):
        return delta_rows(e, (own_chip, core_chip), chip_plan, width)

    def plane_rows(e):
        return delta_rows(e, (own_plane, core_plane, *cross_parts), plane_plan, width)

    def arrived(chip, plane):
        here, first, here_cross, first_cross = chip
        second, third = plane
        return [here, swap(first, 4), swap(second, 8), swap(third, 12), swap(here_cross, 2), swap(first_cross, 6)]

    cross_low, both_low = swap(low, 2), swap(low, 3)
    chip = jnp.concatenate([low, swap(low, 1)], axis=1)
    by_chip = chip_rows(chip[: ROOMS[0]])
    by_chip, cross_low, both_low = lax.optimization_barrier((by_chip, cross_low, both_low))
    plane = jnp.concatenate([chip, cross_low, both_low], axis=1)
    by_plane = plane_rows(plane[: ROOMS[0]])
    by_plane, x_parts = lax.optimization_barrier((by_plane, x_parts))
    rows = arrived(by_chip, by_plane)
    gate, up = base(x_parts, gate_matrix, up_matrix, heads)

    def picked(start, room):
        at = jnp.where((ranks >= start) & (ranks < start + room), planes * room + ranks - start, -1)
        pick = (at[:, None] == jnp.arange(PLANES * room, dtype=jnp.int32)[None, :]).astype(BF16)
        return jnp.concatenate([pick, pick[:, : len(ROWS) * room]], axis=1)

    def short():
        return finish(gate, up, first, order, rows)

    def more(room):
        at = slice(ROOMS[0], ROOMS[0] + room)
        rest = arrived(chip_rows(chip[at]), plane_rows(plane[at]))
        pick = jnp.concatenate([first, picked(ROOMS[0], room)], axis=1)
        return finish(gate, up, pick, order, rows + rest)

    return lax.switch(rounds[0], (short, lambda: more(ROOMS[1]), lambda: more(ROOMS[1] + ROOMS[2])))


def solution(mesh):
    in_specs = (
        P(("groups", "dp"), None),
        P(("groups", "dp"), None),
        P(),
        P(None, "dp"),
        P(None, "dp"),
        P("dp", None, None),
        P("dp", None, None),
    )
    out_specs = P("groups", "dp")
    shards = plane_shards if mesh.shape["dp"] == 16 and mesh.shape["groups"] == 2 else general_shards
    return jax.shard_map(shards, mesh=mesh, in_specs=in_specs, out_specs=out_specs, check_vma=False)
```

profile of v0, /device:TPU:0, one launch (start us, length us, event | category | flops | bytes accessed | tf_op | source)
XLA Modules:
  0.0 63.2 jit_solution(10266488229726147064)
XLA Ops:
  0.0 0.7 %convert_bitcast_fusion = bf16[8]{0:T(256)(128)(2,1)S(1)} fusion(s32[8,1]{0,1:T(1,128)} %param.12), kind=kLoop, calls=%fused_computation.23 | loop fusion | flops 8 | bytes 48 | tf_op jit(solution)/shard_map/broadcast_in_dim | solution.py:395
  0.7 1.1 %cut_cross.1 = (bf16[32,3584]{1,0:T(8,128)(2,1)S(1)}, bf16[32,3584]{1,0:T(8,128)(2,1)S(1)}) custom-call(bf16[64,28672]{1,0:T(8,128)(2,1)} %bitcast.14), custom_call_target="tpu_custom_call" | custom-call | bytes 917504 | tf_op jit(solution)/shard_map/cut_cross/pallas_call | solution.py:103
  1.9 3.0 %collective-permute-start.10 = (bf16[8,8320]{1,0:T(8,128)(2,1)S(1)}, bf16[8,8320]{1,0:T(8,128)(2,1)S(1)}, u32[]{:S(2)}, u32[]{:S(2)}) collective-permute-start(bf16[8,8320]{1,0:T(8,128)(2,1)S(1)} %pad_maximum_fusion.6), channel_id=1, source_target_pairs={{0,2},{1,3},{2,0},{3,1},{4,6},{5,7},{6,4},{7,5},{8,10},{9,11},{10,... | collective-permute-start | bytes 399368 | tf_op jit(solution)/shard_map/ppermute | solution.py:390
  4.9 3.6 %collective-permute-start.12 = (bf16[8,8320]{1,0:T(8,128)(2,1)S(1)}, bf16[8,8320]{1,0:T(8,128)(2,1)S(1)}, u32[]{:S(2)}, u32[]{:S(2)}) collective-permute-start(bf16[8,8320]{1,0:T(8,128)(2,1)S(1)} %pad_maximum_fusion.6), channel_id=1, source_target_pairs={{0,12},{1,13},{2,14},{3,15},{4,8},{5,9},{6,10},{7,11},{8,4},{9,5},... | collective-permute-start | bytes 399368 | tf_op jit(solution)/shard_map/ppermute | solution.py:390
  9.1 1.9 %repack.1 = (bf16[64,7168]{1,0:T(8,128)(2,1)S(1)}, bf16[64,3584]{1,0:T(8,128)(2,1)S(1)}, bf16[64,7168]{1,0:T(8,128)(2,1)S(1)}, bf16[64,3584]{1,0:T(8,128)(2,1)S(1)}) custom-call(bf16[64,28672]{1,0:T(8,128)(2,1)} %bitcast.15), custom_call_target="tpu_custom_call" | custom-call | bytes 5505024 | tf_op jit(solution)/shard_map/repack/pallas_call | solution.py:133
  11.1 3.1 %fetch.2.refs_6_ = bf16[2048,1792]{1,0:T(8,128)(2,1)S(1)} custom-call(bf16[64,3584]{1,0:T(8,128)(2,1)S(1)} %get-tuple-element.227.after_ref.refs_0_, bf16[8192,1792]{1,0:T(8,128)(2,1)} %refs_4_.1), custom_call_target="tpu_custom_call" | custom-call | bytes 29360128 | tf_op jit(solution)/shard_map/fetch/pallas_call | solution.py:253
  14.2 1.6 %collective-permute-start.14 = (bf16[64,3584]{1,0:T(8,128)(2,1)S(1)}, bf16[64,3584]{1,0:T(8,128)(2,1)S(1)}, u32[]{:S(2)}, u32[]{:S(2)}) collective-permute-start(bf16[64,3584]{1,0:T(8,128)(2,1)S(1)} %get-tuple-element.226), channel_id=1, source_target_pairs={{0,1},{1,0},{2,3},{3,2},{4,5},{5,4},{6,7},{7,6},{8,9},{9,8},{10,11... | collective-permute-start | bytes 1376264 | tf_op jit(solution)/shard_map/ppermute | solution.py:390
  15.9 3.6 %collective-permute-done.11 = bf16[8,8320]{1,0:T(8,128)(2,1)S(1)} collective-permute-done((bf16[8,8320]{1,0:T(8,128)(2,1)S(1)}, bf16[8,8320]{1,0:T(8,128)(2,1)S(1)}, u32[]{:S(2)}, u32[]{:S(2)}) %collective-permute-start.11) | collective-permute-done | bytes 133152 | tf_op jit(solution)/shard_map/ppermute | solution.py:390
  19.5 0.6 collective-permute-start.16
  20.1 1.1 %collective-permute-start.15 = (bf16[16,8320]{1,0:T(8,128)(2,1)S(1)}, bf16[16,8320]{1,0:T(8,128)(2,1)S(1)}, u32[]{:S(2)}, u32[]{:S(2)}) collective-permute-start(bf16[16,8320]{1,0:T(8,128)(2,1)S(1)} %pad_maximum_fusion.4.after_ref), channel_id=1, source_target_pairs={{0,4},{1,5},{2,6},{3,7},{4,0},{5,1},{6,2},{7,3},{8,12},{9,13},{10,... | collective-permute-start | bytes 798728 | tf_op jit(solution)/shard_map/ppermute | solution.py:390
  21.2 3.1 %fetch.3.refs_7_ = bf16[2048,1792]{1,0:T(8,128)(2,1)S(1)} custom-call(bf16[16,8320]{1,0:T(8,128)(2,1)S(1)} %pad_maximum_fusion.4.after_ref, bf16[8192,1792]{1,0:T(8,128)(2,1)} %refs_5_.1), custom_call_target="tpu_custom_call" | custom-call | bytes 29360128 | tf_op jit(solution)/shard_map/fetch/pallas_call | solution.py:253
  24.4 2.8 %collective-permute-done.16 = bf16[16,8320]{1,0:T(8,128)(2,1)S(1)} collective-permute-done((bf16[16,8320]{1,0:T(8,128)(2,1)S(1)}, bf16[16,8320]{1,0:T(8,128)(2,1)S(1)}, u32[]{:S(2)}, u32[]{:S(2)}) %collective-permute-start.16) | collective-permute-done | bytes 266272 | tf_op jit(solution)/shard_map/ppermute | solution.py:390
  28.2 1.6 %collective-permute-start.24 = (bf16[64,3584]{1,0:T(8,128)(2,1)S(1)}, bf16[64,3584]{1,0:T(8,128)(2,1)S(1)}, u32[]{:S(2)}, u32[]{:S(2)}) collective-permute-start(bf16[64,3584]{1,0:T(8,128)(2,1)S(1)} %constant_dynamic-update-slice_fusion.refs_2_), channel_id=1, source_target_pairs={{0,16},{16,0},{1,17},{17,1},{2,18},{18,2},{3,19},{19,3},{4,20},{20... | collective-permute-start | bytes 1376264 | tf_op jit(solution)/shard_map/ppermute | solution.py:393
  30.4 1.2 %low_rows.1 = (bf16[128,64]{1,0:T(8,128)(2,1)S(1)}, s32[2,128]{1,0:T(2,128)S(1)}, bf16[128,384]{1,0:T(8,128)(2,1)S(1)}, bf16[128,128]{1,0:T(8,128)(2,1)S(1)}, s32[1]{0:T(128)}) custom-call(bf16[32,8320]{1,0:T(8,128)(2,1)S(1)} %pad_maximum_fusion.2.refs_0_, bf16[32,8320]{1,0:T(8,128)(2,1)S(1)} %pad_maximum_fusion.3.refs_1_, ...), custom_call_target="tpu_custom_call" | custom-call | bytes 4096 | tf_op jit(solution)/shard_map/low_rows/pallas_call | solution.py:191
  31.8 1.5 %collective-permute-start.23 = (bf16[128,64]{1,0:T(8,128)(2,1)S(1)}, bf16[128,64]{1,0:T(8,128)(2,1)S(1)}, u32[]{:S(2)}, u32[]{:S(2)}) collective-permute-start(bf16[128,64]{1,0:T(8,128)(2,1)S(1)} %get-tuple-element.238), channel_id=1, source_target_pairs={{0,3},{1,2},{2,1},{3,0},{4,7},{5,6},{6,5},{7,4},{8,11},{9,10},{10,... | collective-permute-start | bytes 49160 | tf_op jit(solution)/shard_map/ppermute | solution.py:390
  35.1 2.0 %collective-permute-done.22 = bf16[128,64]{1,0:T(8,128)(2,1)S(1)} collective-permute-done((bf16[128,64]{1,0:T(8,128)(2,1)S(1)}, bf16[128,64]{1,0:T(8,128)(2,1)S(1)}, u32[]{:S(2)}, u32[]{:S(2)}) %collective-permute-start.22) | collective-permute-done | bytes 16416 | tf_op jit(solution)/shard_map/ppermute | solution.py:390
  37.3 1.8 %collective-permute-start.25 = (bf16[64,1792]{1,0:T(8,128)(2,1)S(1)}, bf16[64,1792]{1,0:T(8,128)(2,1)S(1)}, u32[]{:S(2)}, u32[]{:S(2)}) collective-permute-start(bf16[64,1792]{1,0:T(8,128)(2,1)S(1)} %get-tuple-element.263), channel_id=1, source_target_pairs={{0,4},{1,5},{2,6},{3,7},{4,0},{5,1},{6,2},{7,3},{8,12},{9,13},{10,... | collective-permute-start | bytes 688136 | tf_op jit(solution)/shard_map/ppermute | solution.py:390
  39.6 1.2 %collective-permute-start.29 = (bf16[64,1792]{1,0:T(8,128)(2,1)S(1)}, bf16[64,1792]{1,0:T(8,128)(2,1)S(1)}, u32[]{:S(2)}, u32[]{:S(2)}) collective-permute-start(bf16[64,1792]{1,0:T(8,128)(2,1)S(1)} %get-tuple-element.267), channel_id=1, source_target_pairs={{0,6},{1,7},{2,4},{3,5},{4,2},{5,3},{6,0},{7,1},{8,14},{9,15},{10,... | collective-permute-start | bytes 688136 | tf_op jit(solution)/shard_map/ppermute | solution.py:390
  41.4 3.2 %collective-permute-start.26 = (bf16[64,1792]{1,0:T(8,128)(2,1)S(1)}, bf16[64,1792]{1,0:T(8,128)(2,1)S(1)}, u32[]{:S(2)}, u32[]{:S(2)}) collective-permute-start(bf16[64,1792]{1,0:T(8,128)(2,1)S(1)} %get-tuple-element.264), channel_id=1, source_target_pairs={{0,8},{1,9},{2,10},{3,11},{4,12},{5,13},{6,14},{7,15},{8,0},{9,1},... | collective-permute-start | bytes 688136 | tf_op jit(solution)/shard_map/ppermute | solution.py:390
  44.6 0.9 %collective-permute-start.27 = (bf16[64,1792]{1,0:T(8,128)(2,1)S(1)}, bf16[64,1792]{1,0:T(8,128)(2,1)S(1)}, u32[]{:S(2)}, u32[]{:S(2)}) collective-permute-start(bf16[64,1792]{1,0:T(8,128)(2,1)S(1)} %get-tuple-element.265), channel_id=1, source_target_pairs={{0,12},{1,13},{2,14},{3,15},{4,8},{5,9},{6,10},{7,11},{8,4},{9,5},... | collective-permute-start | bytes 688136 | tf_op jit(solution)/shard_map/ppermute | solution.py:390
  45.6 14.5 %base.1 = (f32[128,1792]{1,0:T(8,128)S(1)}, f32[128,1792]{1,0:T(8,128)S(1)}) custom-call(bf16[32,8320]{1,0:T(8,128)(2,1)S(1)} %pad_maximum_fusion.2.refs_0_, bf16[32,8320]{1,0:T(8,128)(2,1)S(1)} %pad_maximum_fusion.3.refs_1_, bf16[32,8320]{1,0:T(8,128)(2,1)S(1)} %collective-permute-done.19.refs_2_, bf16[32,8320]{1,0:T(8,128)(2,1)S(1)} %collective-permute-done.20.refs_3_, ...), custom_call_target="tpu_custom_call" | custom-call | flops 7516192768 | bytes 58720256 | tf_op jit(solution)/shard_map/base/pallas_call | solution.py:318
  60.2 1.4 %collective-permute-done.27 = bf16[64,1792]{1,0:T(8,128)(2,1)S(1)} collective-permute-done((bf16[64,1792]{1,0:T(8,128)(2,1)S(1)}, bf16[64,1792]{1,0:T(8,128)(2,1)S(1)}, u32[]{:S(2)}, u32[]{:S(2)}) %collective-permute-start.27) | collective-permute-done | bytes 229408 | tf_op jit(solution)/shard_map/ppermute | solution.py:390
  61.6 1.6 %conditional.1 = (bf16[128,1792]{1,0:T(8,128)(2,1)}) conditional(s32[]{:T(128)} %bitcast.7, (f32[128,1792]{1,0:T(8,128)S(1)}, f32[128,1792]{1,0:T(8,128)S(1)}, bf16[128,384]{1,0:T(8,128)(2,1)S(1)}, bf16[128,128]{1,0:T(8,128)(2,1)S(1)}, bf16[64,1792]{1,0:T(8,128)(2,1)S(1)}, /*index=5*/bf16[64,1792]{1,0:T(8,128)(2,1)S(1)}, ...), branch_computations={%region_0.1_spmd, %region_1.2_spmd, %region_2.3_spmd} | conditional | flops 656256 | bytes 8890576 | solution.py:468
  61.6 1.6 %finish.3 = bf16[128,1792]{1,0:T(8,128)(2,1)} custom-call(f32[128,1792]{1,0:T(8,128)S(1)} %get-tuple-element.115.gate_ref, f32[128,1792]{1,0:T(8,128)S(1)} %get-tuple-element.116.up_ref, bf16[128,384]{1,0:T(8,128)(2,1)S(1)} %get-tuple-element.117.pick_ref, bf16[128,128]{1,0:T(8,128)(2,1)S(1)} %get-tuple-element.118.order_ref, ...), custom_call_target="tpu_custom_call" | custom-call | bytes 3670016 | tf_op jit(solution)/shard_map/cond/branch_0_fun/finish/pallas_call | solution.py:357
  (50 shorter events, 5.2 us)
Async XLA Ops:
  1.9 12.3 %collective-permute-start.10 = (bf16[8,8320]{1,0:T(8,128)(2,1)S(1)}, bf16[8,8320]{1,0:T(8,128)(2,1)S(1)}, u32[]{:S(2)}, u32[]{:S(2)}) collective-permute-start(bf16[8,8320]{1,0:T(8,128)(2,1)S(1)} %pad_maximum_fusion.6), channel_id=1, source_target_pairs={{0,2},{1,3},{2,0},{3,1},{4,6},{5,7},{6,4},{7,5},{8,10},{9,11},{10,... | collective-permute-start | bytes 399368 | tf_op jit(solution)/shard_map/ppermute | solution.py:390
  4.9 10.9 %collective-permute-start.12 = (bf16[8,8320]{1,0:T(8,128)(2,1)S(1)}, bf16[8,8320]{1,0:T(8,128)(2,1)S(1)}, u32[]{:S(2)}, u32[]{:S(2)}) collective-permute-start(bf16[8,8320]{1,0:T(8,128)(2,1)S(1)} %pad_maximum_fusion.6), channel_id=1, source_target_pairs={{0,12},{1,13},{2,14},{3,15},{4,8},{5,9},{6,10},{7,11},{8,4},{9,5},... | collective-permute-start | bytes 399368 | tf_op jit(solution)/shard_map/ppermute | solution.py:390
  8.5 11.0 %collective-permute-start.11 = (bf16[8,8320]{1,0:T(8,128)(2,1)S(1)}, bf16[8,8320]{1,0:T(8,128)(2,1)S(1)}, u32[]{:S(2)}, u32[]{:S(2)}) collective-permute-start(bf16[8,8320]{1,0:T(8,128)(2,1)S(1)} %pad_maximum_fusion.6), channel_id=1, source_target_pairs={{0,8},{1,9},{2,10},{3,11},{4,12},{5,13},{6,14},{7,15},{8,0},{9,1},... | collective-permute-start | bytes 399368 | tf_op jit(solution)/shard_map/ppermute | solution.py:390
  8.5 15.8 %collective-permute-start.17 = (bf16[32,3584]{1,0:T(8,128)(2,1)S(1)}, bf16[32,3584]{1,0:T(8,128)(2,1)S(1)}, u32[]{:S(2)}, u32[]{:S(2)}) collective-permute-start(bf16[32,3584]{1,0:T(8,128)(2,1)S(1)} %get-tuple-element.231), channel_id=1, source_target_pairs={{0,2},{1,3},{2,0},{3,1},{4,6},{5,7},{6,4},{7,5},{8,10},{9,11},{10,... | collective-permute-start | bytes 688136 | tf_op jit(solution)/shard_map/ppermute | solution.py:390
  9.0 15.3 %collective-permute-start.18 = (bf16[32,3584]{1,0:T(8,128)(2,1)S(1)}, bf16[32,3584]{1,0:T(8,128)(2,1)S(1)}, u32[]{:S(2)}, u32[]{:S(2)}) collective-permute-start(bf16[32,3584]{1,0:T(8,128)(2,1)S(1)} %get-tuple-element.232), channel_id=1, source_target_pairs={{0,3},{1,2},{2,1},{3,0},{4,7},{5,6},{6,5},{7,4},{8,11},{9,10},{10,... | collective-permute-start | bytes 688136 | tf_op jit(solution)/shard_map/ppermute | solution.py:390
  14.2 5.3 %collective-permute-start.14 = (bf16[64,3584]{1,0:T(8,128)(2,1)S(1)}, bf16[64,3584]{1,0:T(8,128)(2,1)S(1)}, u32[]{:S(2)}, u32[]{:S(2)}) collective-permute-start(bf16[64,3584]{1,0:T(8,128)(2,1)S(1)} %get-tuple-element.226), channel_id=1, source_target_pairs={{0,1},{1,0},{2,3},{3,2},{4,5},{5,4},{6,7},{7,6},{8,9},{9,8},{10,11... | collective-permute-start | bytes 1376264 | tf_op jit(solution)/shard_map/ppermute | solution.py:390
  15.8 3.7 %collective-permute-start.13 = (bf16[64,7168]{1,0:T(8,128)(2,1)S(1)}, bf16[64,7168]{1,0:T(8,128)(2,1)S(1)}, u32[]{:S(2)}, u32[]{:S(2)}) collective-permute-start(bf16[64,7168]{1,0:T(8,128)(2,1)S(1)} %get-tuple-element.225), channel_id=1, source_target_pairs={{0,1},{1,0},{2,3},{3,2},{4,5},{5,4},{6,7},{7,6},{8,9},{9,8},{10,11... | collective-permute-start | bytes 2752520 | tf_op jit(solution)/shard_map/ppermute | solution.py:390
  19.5 7.7 %collective-permute-start.16 = (bf16[16,8320]{1,0:T(8,128)(2,1)S(1)}, bf16[16,8320]{1,0:T(8,128)(2,1)S(1)}, u32[]{:S(2)}, u32[]{:S(2)}) collective-permute-start(bf16[16,8320]{1,0:T(8,128)(2,1)S(1)} %pad_maximum_fusion.5), channel_id=1, source_target_pairs={{0,2},{1,3},{2,0},{3,1},{4,6},{5,7},{6,4},{7,5},{8,10},{9,11},{10,... | collective-permute-start | bytes 798728 | tf_op jit(solution)/shard_map/ppermute | solution.py:390
  20.1 7.5 %collective-permute-start.15 = (bf16[16,8320]{1,0:T(8,128)(2,1)S(1)}, bf16[16,8320]{1,0:T(8,128)(2,1)S(1)}, u32[]{:S(2)}, u32[]{:S(2)}) collective-permute-start(bf16[16,8320]{1,0:T(8,128)(2,1)S(1)} %pad_maximum_fusion.4.after_ref), channel_id=1, source_target_pairs={{0,4},{1,5},{2,6},{3,7},{4,0},{5,1},{6,2},{7,3},{8,12},{9,13},{10,... | collective-permute-start | bytes 798728 | tf_op jit(solution)/shard_map/ppermute | solution.py:390
  24.3 5.5 %copy-start.4 = (s32[16]{0:T(128)S(1)}, s32[16]{0:T(128)}, u32[]{:S(2)}) copy-start(s32[16]{0:T(128)} %param.13) | copy-start | bytes 196
  24.3 6.1 %copy-start = (bf16[1,8192,64]{1,2,0:T(8,128)(2,1)S(1)}, bf16[1,8192,64]{1,2,0:T(8,128)(2,1)}, u32[]{:S(2)}) copy-start(bf16[1,8192,64]{1,2,0:T(8,128)(2,1)} %param.16) | copy-start | bytes 3145732
  24.4 6.0 %copy-start.1 = (s32[128,1]{1,0:T(8,128)S(1)}, s32[128,1]{1,0:T(8,128)}, u32[]{:S(2)}) copy-start(s32[128,1]{1,0:T(8,128)} %constant.35.refs_7_) | copy-start | bytes 1540
  24.4 6.0 %copy-start.2 = (s32[1,128]{1,0:T(1,128)S(1)}, s32[1,128]{1,0:T(1,128)}, u32[]{:S(2)}) copy-start(s32[1,128]{1,0:T(1,128)} %constant.34.refs_6_) | copy-start | bytes 1540
  27.7 2.2 %collective-permute-start.19 = (bf16[32,8320]{1,0:T(8,128)(2,1)S(1)}, bf16[32,8320]{1,0:T(8,128)(2,1)S(1)}, u32[]{:S(2)}, u32[]{:S(2)}) collective-permute-start(bf16[32,8320]{1,0:T(8,128)(2,1)S(1)} %pad_maximum_fusion.2.refs_0_), channel_id=1, source_target_pairs={{0,1},{1,0},{2,3},{3,2},{4,5},{5,4},{6,7},{7,6},{8,9},{9,8},{10,11... | collective-permute-start | bytes 1597448 | tf_op jit(solution)/shard_map/ppermute | solution.py:390
  27.7 2.7 %collective-permute-start.20 = (bf16[32,8320]{1,0:T(8,128)(2,1)S(1)}, bf16[32,8320]{1,0:T(8,128)(2,1)S(1)}, u32[]{:S(2)}, u32[]{:S(2)}) collective-permute-start(bf16[32,8320]{1,0:T(8,128)(2,1)S(1)} %pad_maximum_fusion.3.refs_1_), channel_id=1, source_target_pairs={{0,1},{1,0},{2,3},{3,2},{4,5},{5,4},{6,7},{7,6},{8,9},{9,8},{10,11... | collective-permute-start | bytes 1597448 | tf_op jit(solution)/shard_map/ppermute | solution.py:390
  28.2 12.6 %collective-permute-start.24 = (bf16[64,3584]{1,0:T(8,128)(2,1)S(1)}, bf16[64,3584]{1,0:T(8,128)(2,1)S(1)}, u32[]{:S(2)}, u32[]{:S(2)}) collective-permute-start(bf16[64,3584]{1,0:T(8,128)(2,1)S(1)} %constant_dynamic-update-slice_fusion.refs_2_), channel_id=1, source_target_pairs={{0,16},{16,0},{1,17},{17,1},{2,18},{18,2},{3,19},{19,3},{4,20},{20... | collective-permute-start | bytes 1376264 | tf_op jit(solution)/shard_map/ppermute | solution.py:393
  31.6 2.9 %collective-permute-start.21 = (bf16[128,64]{1,0:T(8,128)(2,1)S(1)}, bf16[128,64]{1,0:T(8,128)(2,1)S(1)}, u32[]{:S(2)}, u32[]{:S(2)}) collective-permute-start(bf16[128,64]{1,0:T(8,128)(2,1)S(1)} %get-tuple-element.238), channel_id=1, source_target_pairs={{0,1},{1,0},{2,3},{3,2},{4,5},{5,4},{6,7},{7,6},{8,9},{9,8},{10,11... | collective-permute-start | bytes 49160 | tf_op jit(solution)/shard_map/ppermute | solution.py:390
  31.8 3.4 %collective-permute-start.23 = (bf16[128,64]{1,0:T(8,128)(2,1)S(1)}, bf16[128,64]{1,0:T(8,128)(2,1)S(1)}, u32[]{:S(2)}, u32[]{:S(2)}) collective-permute-start(bf16[128,64]{1,0:T(8,128)(2,1)S(1)} %get-tuple-element.238), channel_id=1, source_target_pairs={{0,3},{1,2},{2,1},{3,0},{4,7},{5,6},{6,5},{7,4},{8,11},{9,10},{10,... | collective-permute-start | bytes 49160 | tf_op jit(solution)/shard_map/ppermute | solution.py:390
  33.3 3.9 %collective-permute-start.22 = (bf16[128,64]{1,0:T(8,128)(2,1)S(1)}, bf16[128,64]{1,0:T(8,128)(2,1)S(1)}, u32[]{:S(2)}, u32[]{:S(2)}) collective-permute-start(bf16[128,64]{1,0:T(8,128)(2,1)S(1)} %get-tuple-element.238), channel_id=1, source_target_pairs={{0,2},{1,3},{2,0},{3,1},{4,6},{5,7},{6,4},{7,5},{8,10},{9,11},{10,... | collective-permute-start | bytes 49160 | tf_op jit(solution)/shard_map/ppermute | solution.py:390
  37.3 22.9 %collective-permute-start.25 = (bf16[64,1792]{1,0:T(8,128)(2,1)S(1)}, bf16[64,1792]{1,0:T(8,128)(2,1)S(1)}, u32[]{:S(2)}, u32[]{:S(2)}) collective-permute-start(bf16[64,1792]{1,0:T(8,128)(2,1)S(1)} %get-tuple-element.263), channel_id=1, source_target_pairs={{0,4},{1,5},{2,6},{3,7},{4,0},{5,1},{6,2},{7,3},{8,12},{9,13},{10,... | collective-permute-start | bytes 688136 | tf_op jit(solution)/shard_map/ppermute | solution.py:390
  39.1 21.1 %collective-permute-start.28 = (bf16[64,1792]{1,0:T(8,128)(2,1)S(1)}, bf16[64,1792]{1,0:T(8,128)(2,1)S(1)}, u32[]{:S(2)}, u32[]{:S(2)}) collective-permute-start(bf16[64,1792]{1,0:T(8,128)(2,1)S(1)} %get-tuple-element.266), channel_id=1, source_target_pairs={{0,2},{1,3},{2,0},{3,1},{4,6},{5,7},{6,4},{7,5},{8,10},{9,11},{10,... | collective-permute-start | bytes 688136 | tf_op jit(solution)/shard_map/ppermute | solution.py:390
  39.6 20.5 %collective-permute-start.29 = (bf16[64,1792]{1,0:T(8,128)(2,1)S(1)}, bf16[64,1792]{1,0:T(8,128)(2,1)S(1)}, u32[]{:S(2)}, u32[]{:S(2)}) collective-permute-start(bf16[64,1792]{1,0:T(8,128)(2,1)S(1)} %get-tuple-element.267), channel_id=1, source_target_pairs={{0,6},{1,7},{2,4},{3,5},{4,2},{5,3},{6,0},{7,1},{8,14},{9,15},{10,... | collective-permute-start | bytes 688136 | tf_op jit(solution)/shard_map/ppermute | solution.py:390
  41.4 18.8 %collective-permute-start.26 = (bf16[64,1792]{1,0:T(8,128)(2,1)S(1)}, bf16[64,1792]{1,0:T(8,128)(2,1)S(1)}, u32[]{:S(2)}, u32[]{:S(2)}) collective-permute-start(bf16[64,1792]{1,0:T(8,128)(2,1)S(1)} %get-tuple-element.264), channel_id=1, source_target_pairs={{0,8},{1,9},{2,10},{3,11},{4,12},{5,13},{6,14},{7,15},{8,0},{9,1},... | collective-permute-start | bytes 688136 | tf_op jit(solution)/shard_map/ppermute | solution.py:390
  44.6 17.0 %collective-permute-start.27 = (bf16[64,1792]{1,0:T(8,128)(2,1)S(1)}, bf16[64,1792]{1,0:T(8,128)(2,1)S(1)}, u32[]{:S(2)}, u32[]{:S(2)}) collective-permute-start(bf16[64,1792]{1,0:T(8,128)(2,1)S(1)} %get-tuple-element.265), channel_id=1, source_target_pairs={{0,12},{1,13},{2,14},{3,15},{4,8},{5,9},{6,10},{7,11},{8,4},{9,5},... | collective-permute-start | bytes 688136 | tf_op jit(solution)/shard_map/ppermute | solution.py:390
  (1 other events, 1.2 us)
where the time goes:
time: 63.8 us; the launch traced here: 63.2 us
  Pallas kernels  27.4 us (43%)
  starting transfers between devices  22.6 us (35%)
  waiting for transfers between devices  11 us (17%)
  other arithmetic  1.09 us (2%)
  between operations  0.89 us (1%)
    ppermute x19, starting transfers between devices, swap(): return lax.ppermute(value, 'dp', [(d, d ^ k) for d in range(count)])  21.1 us
    pallas_call x1, Pallas kernels, base(): pl.pallas_call(functools.partial(base_kernel, steps, rows), out_shape=[sh...  14.5 us
    ppermute x19, waiting for transfers between devices, swap(): return lax.ppermute(value, 'dp', [(d, d ^ k) for d in range(count)])  11 us
    pallas_call x2, Pallas kernels, fetch(): pl.pallas_call(functools.partial(fetch_kernel, 0), out_shape=shape, in_sp...  6.19 us
    pallas_call x1, Pallas kernels, repack(): pl.pallas_call(functools.partial(repack_kernel, width), out_shape=[for_ro...  1.94 us
    ppermute x1, starting transfers between devices, other(): return lax.ppermute(value, 'groups', [(0, 1), (1, 0)])  1.58 us
    pallas_call x1, Pallas kernels, finish(): pl.pallas_call(functools.partial(finish_kernel, width // n), out_shape=pl...  1.56 us
  transfers between devices with their start and end apart: 20, of which 7 were waited for; matrix products, arithmetic and copies ran while one was open for 1% of the time, Pallas kernels for 39%

commit v1 on v0

--- a/solution.py
+++ b/solution.py
@@ -210,6 +210,7 @@
     e = e_ref[...]
     chip = 2 * parts[0].shape[0]
     if e.shape[1] > chip:
+        parts = (*parts[:-2], jnp.concatenate([parts[-2][...], parts[-1][...]], axis=1))
         shape = (e.shape[1] - chip,) * 2
         half = jnp.broadcast_to(lax.axis_index("groups") * (chip // 4), shape)
         here, there = lax.broadcasted_iota(jnp.int32, shape, 0), lax.broadcasted_iota(jnp.int32, shape, 1)
@@ -392,31 +393,31 @@
     def other(value):
         return lax.ppermute(value, "groups", [(0, 1), (1, 0)])
 
-    ids = jnp.broadcast_to(token_adapter_index.astype(BF16), (own_rows, LANES))
+    index, cross, both = lax.optimization_barrier((token_adapter_index, *cut_cross(up_factor, width)))
+    ids = jnp.broadcast_to(index.astype(BF16), (own_rows, LANES))
     packed = jnp.concatenate([tokens, ids], axis=1)
-    packed, cross, both = lax.optimization_barrier((packed, *cut_cross(up_factor, width)))
     cross, both = swap(cross, 2), swap(both, 3)
     second, third = swap(packed, 8), swap(packed, 12)
     pair = jnp.concatenate([packed, swap(packed, 2)], axis=0)
     remote = jnp.concatenate([second, third], axis=0)
     own_chip, own_plane, core_chip, core_plane = repack(up_factor, width)
+    gate_head = fetch(own_plane, gate_matrix)
+    close = jnp.concatenate([pair, swap(pair, 4)], axis=0)
+    remote, down, core_chip, core_plane, gate_head, cross, both = lax.optimization_barrier(
+        (remote, adapter_down_factor[0], core_chip, core_plane, gate_head, cross, both)
+    )
+    crossed = jnp.concatenate([cross, both], axis=0)
+    part = width * 3 // 7 // LANES * LANES
+    from_group = other(crossed[:, :part])
+    remote = jnp.concatenate([remote, swap(remote, 2)], axis=0)
     core_chip, core_plane = swap(core_chip, 1), swap(core_plane, 1)
-    gate_head = fetch(own_plane, gate_matrix)
-    pair, remote, down, core_chip, core_plane, gate_head = lax.optimization_barrier(
-        (pair, remote, adapter_down_factor[0], core_chip, core_plane, gate_head)
-    )
-    close = jnp.concatenate([pair, swap(pair, 4)], axis=0)
-    remote = jnp.concatenate([remote, swap(remote, 2)], axis=0)
-    up_head = fetch(pair, up_matrix)
-    cross, both, up_head = lax.optimization_barrier((cross, both, up_head))
-    crossed = jnp.concatenate([cross, both], axis=0)
-    heads = (gate_head, up_head)
-    close, remote, heads = lax.optimization_barrier((close, remote, heads))
+    heads = (gate_head, fetch(crossed, up_matrix))
+    close, remote, heads, from_group = lax.optimization_barrier((close, remote, heads, from_group))
     x_parts = (close, remote, swap(close, 1), swap(remote, 1))
     distances = [0, 2, 4, 6, 8, 12, 10, 14]
     distances = distances + [k + 1 for k in distances]
 
-    cross_parts = (crossed, other(crossed))
+    cross_parts = (crossed, from_group, other(crossed[:, part:]))
     half = rank // 2
 
     distance = jnp.array([k for k in distances for _ in range(own_rows)], jnp.int32)
@@ -447,7 +448,7 @@
     by_chip, cross_low, both_low = lax.optimization_barrier((by_chip, cross_low, both_low))
     plane = jnp.concatenate([chip, cross_low, both_low], axis=1)
     by_plane = plane_rows(plane[: ROOMS[0]])
-    by_plane, x_parts = lax.optimization_barrier((by_plane, x_parts))
+    by_plane, by_chip, x_parts = lax.optimization_barrier((by_plane, by_chip, x_parts))
     rows = arrived(by_chip, by_plane)
     gate, up = base(x_parts, gate_matrix, up_matrix, heads)
 

time: 63.8 us -> 63 us (0.987)
  waiting for transfers between devices: 11 us -> 14.2 us
  starting transfers between devices: 22.6 us -> 19.6 us
  other arithmetic: 1.09 us -> 0.41 us
    ppermute x19, starting transfers between devices: 21.1 us -> 16.5 us  [swap(): return lax.ppermute(value, 'dp', [(d, d ^ k) for d in range(count)])]
    ppermute x1 -> x2, waiting for transfers between devices: 0.01 us -> 1.64 us  [other(): return lax.ppermute(value, 'groups', [(0, 1), (1, 0)])]
    ppermute x1 -> x2, starting transfers between devices: 1.58 us -> 3.17 us  [other(): return lax.ppermute(value, 'groups', [(0, 1), (1, 0)])]
    ppermute x19, waiting for transfers between devices: 11 us -> 12.5 us  [swap(): return lax.ppermute(value, 'dp', [(d, d ^ k) for d in range(count)])]
    broadcast_in_dim x1, other arithmetic: 0.66 us -> 0.01 us  [plane_shards(): ids = jnp.broadcast_to(index.astype(BF16), (own_rows, LANES))]
  transfers between devices with their start and end apart: 20 -> 21, of which waited for: 7 -> 7; matrix products, arithmetic and copies ran while one was open for 1% -> 1% of each run, Pallas kernels for 39% -> 39%
where the time goes in v1:
time: 63 us; the launch traced here: 62.8 us
  Pallas kernels  27.4 us (43%)
  starting transfers between devices  19.6 us (31%)
  waiting for transfers between devices  14.2 us (23%)
  between operations  0.93 us (1%)
    ppermute x19, starting transfers between devices, swap(): return lax.ppermute(value, 'dp', [(d, d ^ k) for d in range(count)])  16.5 us
    pallas_call x1, Pallas kernels, base(): pl.pallas_call(functools.partial(base_kernel, steps, rows), out_shape=[sh...  14.5 us
    ppermute x19, waiting for transfers between devices, swap(): return lax.ppermute(value, 'dp', [(d, d ^ k) for d in range(count)])  12.5 us
    pallas_call x2, Pallas kernels, fetch(): pl.pallas_call(functools.partial(fetch_kernel, 0), out_shape=shape, in_sp...  6.19 us
    ppermute x2, starting transfers between devices, other(): return lax.ppermute(value, 'groups', [(0, 1), (1, 0)])  3.17 us
    pallas_call x1, Pallas kernels, repack(): pl.pallas_call(functools.partial(repack_kernel, width), out_shape=[for_ro...  1.94 us
    ppermute x2, waiting for transfers between devices, other(): return lax.ppermute(value, 'groups', [(0, 1), (1, 0)])  1.64 us
    pallas_call x1, Pallas kernels, finish(): pl.pallas_call(functools.partial(finish_kernel, width // n), out_shape=pl...  1.56 us
  transfers between devices with their start and end apart: 21, of which 7 were waited for; matrix products, arithmetic and copies ran while one was open for 1% of the time, Pallas kernels for 39%

profile of v1, /device:TPU:0, one launch (start us, length us, event | category | flops | bytes accessed | tf_op | source)
XLA Modules:
  0.0 62.8 jit_solution(2461747402627057238)
XLA Ops:
  0.0 1.1 %cut_cross.1 = (bf16[32,3584]{1,0:T(8,128)(2,1)S(1)}, bf16[32,3584]{1,0:T(8,128)(2,1)S(1)}) custom-call(bf16[64,28672]{1,0:T(8,128)(2,1)} %bitcast.14), custom_call_target="tpu_custom_call" | custom-call | bytes 917504 | tf_op jit(solution)/shard_map/cut_cross/pallas_call | solution.py:103
  1.3 3.0 %collective-permute-start.10 = (bf16[8,8320]{1,0:T(8,128)(2,1)S(1)}, bf16[8,8320]{1,0:T(8,128)(2,1)S(1)}, u32[]{:S(2)}, u32[]{:S(2)}) collective-permute-start(bf16[8,8320]{1,0:T(8,128)(2,1)S(1)} %pad_maximum_fusion.6), channel_id=1, source_target_pairs={{0,2},{1,3},{2,0},{3,1},{4,6},{5,7},{6,4},{7,5},{8,10},{9,11},{10,... | collective-permute-start | bytes 399368 | tf_op jit(solution)/shard_map/ppermute | solution.py:391
  4.3 3.6 %collective-permute-start.13 = (bf16[8,8320]{1,0:T(8,128)(2,1)S(1)}, bf16[8,8320]{1,0:T(8,128)(2,1)S(1)}, u32[]{:S(2)}, u32[]{:S(2)}) collective-permute-start(bf16[8,8320]{1,0:T(8,128)(2,1)S(1)} %pad_maximum_fusion.6), channel_id=1, source_target_pairs={{0,12},{1,13},{2,14},{3,15},{4,8},{5,9},{6,10},{7,11},{8,4},{9,5},... | collective-permute-start | bytes 399368 | tf_op jit(solution)/shard_map/ppermute | solution.py:391
  8.5 1.9 %repack.1 = (bf16[64,7168]{1,0:T(8,128)(2,1)S(1)}, bf16[64,3584]{1,0:T(8,128)(2,1)S(1)}, bf16[64,7168]{1,0:T(8,128)(2,1)S(1)}, bf16[64,3584]{1,0:T(8,128)(2,1)S(1)}) custom-call(bf16[64,28672]{1,0:T(8,128)(2,1)} %bitcast.15), custom_call_target="tpu_custom_call" | custom-call | bytes 5505024 | tf_op jit(solution)/shard_map/repack/pallas_call | solution.py:133
  10.4 3.1 %fetch.2.refs_6_ = bf16[2048,1792]{1,0:T(8,128)(2,1)S(1)} custom-call(bf16[64,3584]{1,0:T(8,128)(2,1)S(1)} %get-tuple-element.236.after_ref.refs_0_, bf16[8192,1792]{1,0:T(8,128)(2,1)} %refs_4_.1), custom_call_target="tpu_custom_call" | custom-call | bytes 29360128 | tf_op jit(solution)/shard_map/fetch/pallas_call | solution.py:254
  13.6 0.6 %collective-permute-start.11 = (bf16[16,8320]{1,0:T(8,128)(2,1)S(1)}, bf16[16,8320]{1,0:T(8,128)(2,1)S(1)}, u32[]{:S(2)}, u32[]{:S(2)}) collective-permute-start(bf16[16,8320]{1,0:T(8,128)(2,1)S(1)} %pad_maximum_fusion.4), channel_id=1, source_target_pairs={{0,4},{1,5},{2,6},{3,7},{4,0},{5,1},{6,2},{7,3},{8,12},{9,13},{10,... | collective-permute-start | bytes 798728 | tf_op jit(solution)/shard_map/ppermute | solution.py:391
  14.2 4.7 %collective-permute-done.12 = bf16[8,8320]{1,0:T(8,128)(2,1)S(1)} collective-permute-done((bf16[8,8320]{1,0:T(8,128)(2,1)S(1)}, bf16[8,8320]{1,0:T(8,128)(2,1)S(1)}, u32[]{:S(2)}, u32[]{:S(2)}) %collective-permute-start.12) | collective-permute-done | bytes 133152 | tf_op jit(solution)/shard_map/ppermute | solution.py:391
  19.0 0.6 collective-permute-start.16
  19.6 1.6 %collective-permute-start.17 = (bf16[64,768]{1,0:T(8,128)(2,1)S(1)}, bf16[64,768]{1,0:T(8,128)(2,1)S(1)}, u32[]{:S(2)}, u32[]{:S(2)}) collective-permute-start(bf16[64,768]{1,0:T(8,128)(2,1)S(1)} %slice.50), channel_id=1, source_target_pairs={{0,16},{16,0},{1,17},{17,1},{2,18},{18,2},{3,19},{19,3},{4,20},{20... | collective-permute-start | bytes 294920 | tf_op jit(solution)/shard_map/ppermute | solution.py:394
  21.3 3.1 %fetch.3.refs_7_ = bf16[2048,1792]{1,0:T(8,128)(2,1)S(1)} custom-call(bf16[64,3584]{1,0:T(8,128)(2,1)S(1)} %constant_dynamic-update-slice_fusion.after_ref.refs_2_, bf16[8192,1792]{1,0:T(8,128)(2,1)} %refs_5_.1), custom_call_target="tpu_custom_call" | custom-call | bytes 29360128 | tf_op jit(solution)/shard_map/fetch/pallas_call | solution.py:254
  24.6 3.4 %collective-permute-done.16 = bf16[16,8320]{1,0:T(8,128)(2,1)S(1)} collective-permute-done((bf16[16,8320]{1,0:T(8,128)(2,1)S(1)}, bf16[16,8320]{1,0:T(8,128)(2,1)S(1)}, u32[]{:S(2)}, u32[]{:S(2)}) %collective-permute-start.16) | collective-permute-done | bytes 266272 | tf_op jit(solution)/shard_map/ppermute | solution.py:391
  28.6 1.6 %collective-permute-start.25 = (bf16[64,2816]{1,0:T(8,128)(2,1)S(1)}, bf16[64,2816]{1,0:T(8,128)(2,1)S(1)}, u32[]{:S(2)}, u32[]{:S(2)}) collective-permute-start(bf16[64,2816]{1,0:T(8,128)(2,1)S(1)} %slice.54), channel_id=1, source_target_pairs={{0,16},{16,0},{1,17},{17,1},{2,18},{18,2},{3,19},{19,3},{4,20},{20... | collective-permute-start | bytes 1081352 | tf_op jit(solution)/shard_map/ppermute | solution.py:394
  30.3 0.5 collective-permute-done.19.refs_3_
  30.8 1.2 %low_rows.1 = (bf16[128,64]{1,0:T(8,128)(2,1)S(1)}, s32[2,128]{1,0:T(2,128)S(1)}, bf16[128,384]{1,0:T(8,128)(2,1)S(1)}, bf16[128,128]{1,0:T(8,128)(2,1)S(1)}, s32[1]{0:T(128)}) custom-call(bf16[32,8320]{1,0:T(8,128)(2,1)S(1)} %pad_maximum_fusion.2.refs_0_, bf16[32,8320]{1,0:T(8,128)(2,1)S(1)} %pad_maximum_fusion.3.refs_1_, ...), custom_call_target="tpu_custom_call" | custom-call | bytes 4096 | tf_op jit(solution)/shard_map/low_rows/pallas_call | solution.py:191
  33.4 1.5 %collective-permute-start.22 = (bf16[128,64]{1,0:T(8,128)(2,1)S(1)}, bf16[128,64]{1,0:T(8,128)(2,1)S(1)}, u32[]{:S(2)}, u32[]{:S(2)}) collective-permute-start(bf16[128,64]{1,0:T(8,128)(2,1)S(1)} %get-tuple-element.247), channel_id=1, source_target_pairs={{0,2},{1,3},{2,0},{3,1},{4,6},{5,7},{6,4},{7,5},{8,10},{9,11},{10,... | collective-permute-start | bytes 49160 | tf_op jit(solution)/shard_map/ppermute | solution.py:391
  35.5 1.8 %collective-permute-done.22 = bf16[128,64]{1,0:T(8,128)(2,1)S(1)} collective-permute-done((bf16[128,64]{1,0:T(8,128)(2,1)S(1)}, bf16[128,64]{1,0:T(8,128)(2,1)S(1)}, u32[]{:S(2)}, u32[]{:S(2)}) %collective-permute-start.22) | collective-permute-done | bytes 16416 | tf_op jit(solution)/shard_map/ppermute | solution.py:391
  37.5 1.6 %collective-permute-done.25.refs_4_ = bf16[64,2816]{1,0:T(8,128)(2,1)S(1)} collective-permute-done((bf16[64,2816]{1,0:T(8,128)(2,1)S(1)}, bf16[64,2816]{1,0:T(8,128)(2,1)S(1)}, u32[]{:S(2)}, u32[]{:S(2)}) %collective-permute-start.25) | collective-permute-done | bytes 360480 | tf_op jit(solution)/shard_map/ppermute | solution.py:394
  39.1 0.5 delta_rows.11
  39.7 2.5 %collective-permute-start.27 = (bf16[64,1792]{1,0:T(8,128)(2,1)S(1)}, bf16[64,1792]{1,0:T(8,128)(2,1)S(1)}, u32[]{:S(2)}, u32[]{:S(2)}) collective-permute-start(bf16[64,1792]{1,0:T(8,128)(2,1)S(1)} %get-tuple-element.276), channel_id=1, source_target_pairs={{0,8},{1,9},{2,10},{3,11},{4,12},{5,13},{6,14},{7,15},{8,0},{9,1},... | collective-permute-start | bytes 688136 | tf_op jit(solution)/shard_map/ppermute | solution.py:391
  42.2 1.9 %collective-permute-start.28 = (bf16[64,1792]{1,0:T(8,128)(2,1)S(1)}, bf16[64,1792]{1,0:T(8,128)(2,1)S(1)}, u32[]{:S(2)}, u32[]{:S(2)}) collective-permute-start(bf16[64,1792]{1,0:T(8,128)(2,1)S(1)} %get-tuple-element.277), channel_id=1, source_target_pairs={{0,12},{1,13},{2,14},{3,15},{4,8},{5,9},{6,10},{7,11},{8,4},{9,5},... | collective-permute-start | bytes 688136 | tf_op jit(solution)/shard_map/ppermute | solution.py:391
  44.8 14.5 %base.1 = (f32[128,1792]{1,0:T(8,128)S(1)}, f32[128,1792]{1,0:T(8,128)S(1)}) custom-call(bf16[32,8320]{1,0:T(8,128)(2,1)S(1)} %pad_maximum_fusion.2.refs_0_, bf16[32,8320]{1,0:T(8,128)(2,1)S(1)} %pad_maximum_fusion.3.refs_1_, bf16[32,8320]{1,0:T(8,128)(2,1)S(1)} %collective-permute-done.18.refs_2_, bf16[32,8320]{1,0:T(8,128)(2,1)S(1)} %collective-permute-done.19.refs_3_, ...), custom_call_target="tpu_custom_call" | custom-call | flops 7516192768 | bytes 58720256 | tf_op jit(solution)/shard_map/base/pallas_call | solution.py:319
  59.3 1.9 %collective-permute-done.30 = bf16[64,1792]{1,0:T(8,128)(2,1)S(1)} collective-permute-done((bf16[64,1792]{1,0:T(8,128)(2,1)S(1)}, bf16[64,1792]{1,0:T(8,128)(2,1)S(1)}, u32[]{:S(2)}, u32[]{:S(2)}) %collective-permute-start.30) | collective-permute-done | bytes 229408 | tf_op jit(solution)/shard_map/ppermute | solution.py:391
  61.2 1.6 %conditional.1 = (bf16[128,1792]{1,0:T(8,128)(2,1)}) conditional(s32[]{:T(128)} %bitcast.7, (f32[128,1792]{1,0:T(8,128)S(1)}, f32[128,1792]{1,0:T(8,128)S(1)}, bf16[128,384]{1,0:T(8,128)(2,1)S(1)}, bf16[128,128]{1,0:T(8,128)(2,1)S(1)}, bf16[64,1792]{1,0:T(8,128)(2,1)S(1)}, /*index=5*/bf16[64,1792]{1,0:T(8,128)(2,1)S(1)}, ...), branch_computations={%region_0.1_spmd, %region_1.2_spmd, %region_2.3_spmd} | conditional | flops 656256 | bytes 8890576 | solution.py:469
  61.2 1.6 %finish.3 = bf16[128,1792]{1,0:T(8,128)(2,1)} custom-call(f32[128,1792]{1,0:T(8,128)S(1)} %get-tuple-element.119.gate_ref, f32[128,1792]{1,0:T(8,128)S(1)} %get-tuple-element.120.up_ref, bf16[128,384]{1,0:T(8,128)(2,1)S(1)} %get-tuple-element.121.pick_ref, bf16[128,128]{1,0:T(8,128)(2,1)S(1)} %get-tuple-element.122.order_ref, ...), custom_call_target="tpu_custom_call" | custom-call | bytes 3670016 | tf_op jit(solution)/shard_map/cond/branch_0_fun/finish/pallas_call | solution.py:358
  (56 shorter events, 3.9 us)
Async XLA Ops:
  1.3 12.3 %collective-permute-start.10 = (bf16[8,8320]{1,0:T(8,128)(2,1)S(1)}, bf16[8,8320]{1,0:T(8,128)(2,1)S(1)}, u32[]{:S(2)}, u32[]{:S(2)}) collective-permute-start(bf16[8,8320]{1,0:T(8,128)(2,1)S(1)} %pad_maximum_fusion.6), channel_id=1, source_target_pairs={{0,2},{1,3},{2,0},{3,1},{4,6},{5,7},{6,4},{7,5},{8,10},{9,11},{10,... | collective-permute-start | bytes 399368 | tf_op jit(solution)/shard_map/ppermute | solution.py:391
  4.3 10.0 %collective-permute-start.13 = (bf16[8,8320]{1,0:T(8,128)(2,1)S(1)}, bf16[8,8320]{1,0:T(8,128)(2,1)S(1)}, u32[]{:S(2)}, u32[]{:S(2)}) collective-permute-start(bf16[8,8320]{1,0:T(8,128)(2,1)S(1)} %pad_maximum_fusion.6), channel_id=1, source_target_pairs={{0,12},{1,13},{2,14},{3,15},{4,8},{5,9},{6,10},{7,11},{8,4},{9,5},... | collective-permute-start | bytes 399368 | tf_op jit(solution)/shard_map/ppermute | solution.py:391
  7.9 11.1 %collective-permute-start.12 = (bf16[8,8320]{1,0:T(8,128)(2,1)S(1)}, bf16[8,8320]{1,0:T(8,128)(2,1)S(1)}, u32[]{:S(2)}, u32[]{:S(2)}) collective-permute-start(bf16[8,8320]{1,0:T(8,128)(2,1)S(1)} %pad_maximum_fusion.6), channel_id=1, source_target_pairs={{0,8},{1,9},{2,10},{3,11},{4,12},{5,13},{6,14},{7,15},{8,0},{9,1},... | collective-permute-start | bytes 399368 | tf_op jit(solution)/shard_map/ppermute | solution.py:391
  7.9 11.1 %collective-permute-start.14 = (bf16[32,3584]{1,0:T(8,128)(2,1)S(1)}, bf16[32,3584]{1,0:T(8,128)(2,1)S(1)}, u32[]{:S(2)}, u32[]{:S(2)}) collective-permute-start(bf16[32,3584]{1,0:T(8,128)(2,1)S(1)} %get-tuple-element.237), channel_id=1, source_target_pairs={{0,2},{1,3},{2,0},{3,1},{4,6},{5,7},{6,4},{7,5},{8,10},{9,11},{10,... | collective-permute-start | bytes 688136 | tf_op jit(solution)/shard_map/ppermute | solution.py:391
  8.4 10.6 %collective-permute-start.15 = (bf16[32,3584]{1,0:T(8,128)(2,1)S(1)}, bf16[32,3584]{1,0:T(8,128)(2,1)S(1)}, u32[]{:S(2)}, u32[]{:S(2)}) collective-permute-start(bf16[32,3584]{1,0:T(8,128)(2,1)S(1)} %get-tuple-element.238), channel_id=1, source_target_pairs={{0,3},{1,2},{2,1},{3,0},{4,7},{5,6},{6,5},{7,4},{8,11},{9,10},{10,... | collective-permute-start | bytes 688136 | tf_op jit(solution)/shard_map/ppermute | solution.py:391
  13.6 10.9 %collective-permute-start.11 = (bf16[16,8320]{1,0:T(8,128)(2,1)S(1)}, bf16[16,8320]{1,0:T(8,128)(2,1)S(1)}, u32[]{:S(2)}, u32[]{:S(2)}) collective-permute-start(bf16[16,8320]{1,0:T(8,128)(2,1)S(1)} %pad_maximum_fusion.4), channel_id=1, source_target_pairs={{0,4},{1,5},{2,6},{3,7},{4,0},{5,1},{6,2},{7,3},{8,12},{9,13},{10,... | collective-permute-start | bytes 798728 | tf_op jit(solution)/shard_map/ppermute | solution.py:391
  19.0 9.0 %collective-permute-start.16 = (bf16[16,8320]{1,0:T(8,128)(2,1)S(1)}, bf16[16,8320]{1,0:T(8,128)(2,1)S(1)}, u32[]{:S(2)}, u32[]{:S(2)}) collective-permute-start(bf16[16,8320]{1,0:T(8,128)(2,1)S(1)} %pad_maximum_fusion.5), channel_id=1, source_target_pairs={{0,2},{1,3},{2,0},{3,1},{4,6},{5,7},{6,4},{7,5},{8,10},{9,11},{10,... | collective-permute-start | bytes 798728 | tf_op jit(solution)/shard_map/ppermute | solution.py:391
  19.6 8.4 %collective-permute-start.17 = (bf16[64,768]{1,0:T(8,128)(2,1)S(1)}, bf16[64,768]{1,0:T(8,128)(2,1)S(1)}, u32[]{:S(2)}, u32[]{:S(2)}) collective-permute-start(bf16[64,768]{1,0:T(8,128)(2,1)S(1)} %slice.50), channel_id=1, source_target_pairs={{0,16},{16,0},{1,17},{17,1},{2,18},{18,2},{3,19},{19,3},{4,20},{20... | collective-permute-start | bytes 294920 | tf_op jit(solution)/shard_map/ppermute | solution.py:394
  21.2 13.9 %collective-permute-start.21 = (bf16[64,7168]{1,0:T(8,128)(2,1)S(1)}, bf16[64,7168]{1,0:T(8,128)(2,1)S(1)}, u32[]{:S(2)}, u32[]{:S(2)}) collective-permute-start(bf16[64,7168]{1,0:T(8,128)(2,1)S(1)} %get-tuple-element.249), channel_id=1, source_target_pairs={{0,1},{1,0},{2,3},{3,2},{4,5},{5,4},{6,7},{7,6},{8,9},{9,8},{10,11... | collective-permute-start | bytes 2752520 | tf_op jit(solution)/shard_map/ppermute | solution.py:391
  24.5 6.3 %copy-start = (bf16[1,8192,64]{1,2,0:T(8,128)(2,1)S(1)}, bf16[1,8192,64]{1,2,0:T(8,128)(2,1)}, u32[]{:S(2)}) copy-start(bf16[1,8192,64]{1,2,0:T(8,128)(2,1)} %param.16) | copy-start | bytes 3145732
  24.6 6.2 %copy-start.1 = (s32[128,1]{1,0:T(8,128)S(1)}, s32[128,1]{1,0:T(8,128)}, u32[]{:S(2)}) copy-start(s32[128,1]{1,0:T(8,128)} %constant.35.refs_7_) | copy-start | bytes 1540
  24.6 6.2 %copy-start.2 = (s32[1,128]{1,0:T(1,128)S(1)}, s32[1,128]{1,0:T(1,128)}, u32[]{:S(2)}) copy-start(s32[1,128]{1,0:T(1,128)} %constant.34.refs_6_) | copy-start | bytes 1540
  28.0 2.2 %collective-permute-start.18 = (bf16[32,8320]{1,0:T(8,128)(2,1)S(1)}, bf16[32,8320]{1,0:T(8,128)(2,1)S(1)}, u32[]{:S(2)}, u32[]{:S(2)}) collective-permute-start(bf16[32,8320]{1,0:T(8,128)(2,1)S(1)} %pad_maximum_fusion.2.refs_0_), channel_id=1, source_target_pairs={{0,1},{1,0},{2,3},{3,2},{4,5},{5,4},{6,7},{7,6},{8,9},{9,8},{10,11... | collective-permute-start | bytes 1597448 | tf_op jit(solution)/shard_map/ppermute | solution.py:391
  28.1 2.7 %collective-permute-start.19 = (bf16[32,8320]{1,0:T(8,128)(2,1)S(1)}, bf16[32,8320]{1,0:T(8,128)(2,1)S(1)}, u32[]{:S(2)}, u32[]{:S(2)}) collective-permute-start(bf16[32,8320]{1,0:T(8,128)(2,1)S(1)} %pad_maximum_fusion.3.refs_1_), channel_id=1, source_target_pairs={{0,1},{1,0},{2,3},{3,2},{4,5},{5,4},{6,7},{7,6},{8,9},{9,8},{10,11... | collective-permute-start | bytes 1597448 | tf_op jit(solution)/shard_map/ppermute | solution.py:391
  28.6 10.5 %collective-permute-start.25 = (bf16[64,2816]{1,0:T(8,128)(2,1)S(1)}, bf16[64,2816]{1,0:T(8,128)(2,1)S(1)}, u32[]{:S(2)}, u32[]{:S(2)}) collective-permute-start(bf16[64,2816]{1,0:T(8,128)(2,1)S(1)} %slice.54), channel_id=1, source_target_pairs={{0,16},{16,0},{1,17},{17,1},{2,18},{18,2},{3,19},{19,3},{4,20},{20... | collective-permute-start | bytes 1081352 | tf_op jit(solution)/shard_map/ppermute | solution.py:394
  30.2 8.9 %collective-permute-start.24 = (bf16[64,3584]{1,0:T(8,128)(2,1)S(1)}, bf16[64,3584]{1,0:T(8,128)(2,1)S(1)}, u32[]{:S(2)}, u32[]{:S(2)}) collective-permute-start(bf16[64,3584]{1,0:T(8,128)(2,1)S(1)} %get-tuple-element.256), channel_id=1, source_target_pairs={{0,1},{1,0},{2,3},{3,2},{4,5},{5,4},{6,7},{7,6},{8,9},{9,8},{10,11... | collective-permute-start | bytes 1376264 | tf_op jit(solution)/shard_map/ppermute | solution.py:391
  32.0 1.4 %collective-permute-start.20 = (bf16[128,64]{1,0:T(8,128)(2,1)S(1)}, bf16[128,64]{1,0:T(8,128)(2,1)S(1)}, u32[]{:S(2)}, u32[]{:S(2)}) collective-permute-start(bf16[128,64]{1,0:T(8,128)(2,1)S(1)} %get-tuple-element.247), channel_id=1, source_target_pairs={{0,1},{1,0},{2,3},{3,2},{4,5},{5,4},{6,7},{7,6},{8,9},{9,8},{10,11... | collective-permute-start | bytes 49160 | tf_op jit(solution)/shard_map/ppermute | solution.py:391
  32.2 3.4 %collective-permute-start.23 = (bf16[128,64]{1,0:T(8,128)(2,1)S(1)}, bf16[128,64]{1,0:T(8,128)(2,1)S(1)}, u32[]{:S(2)}, u32[]{:S(2)}) collective-permute-start(bf16[128,64]{1,0:T(8,128)(2,1)S(1)} %get-tuple-element.247), channel_id=1, source_target_pairs={{0,3},{1,2},{2,1},{3,0},{4,7},{5,6},{6,5},{7,4},{8,11},{9,10},{10,... | collective-permute-start | bytes 49160 | tf_op jit(solution)/shard_map/ppermute | solution.py:391
  33.4 4.0 %collective-permute-start.22 = (bf16[128,64]{1,0:T(8,128)(2,1)S(1)}, bf16[128,64]{1,0:T(8,128)(2,1)S(1)}, u32[]{:S(2)}, u32[]{:S(2)}) collective-permute-start(bf16[128,64]{1,0:T(8,128)(2,1)S(1)} %get-tuple-element.247), channel_id=1, source_target_pairs={{0,2},{1,3},{2,0},{3,1},{4,6},{5,7},{6,4},{7,5},{8,10},{9,11},{10,... | collective-permute-start | bytes 49160 | tf_op jit(solution)/shard_map/ppermute | solution.py:391
  39.7 19.6 %collective-permute-start.26 = (bf16[64,1792]{1,0:T(8,128)(2,1)S(1)}, bf16[64,1792]{1,0:T(8,128)(2,1)S(1)}, u32[]{:S(2)}, u32[]{:S(2)}) collective-permute-start(bf16[64,1792]{1,0:T(8,128)(2,1)S(1)} %get-tuple-element.275), channel_id=1, source_target_pairs={{0,4},{1,5},{2,6},{3,7},{4,0},{5,1},{6,2},{7,3},{8,12},{9,13},{10,... | collective-permute-start | bytes 688136 | tf_op jit(solution)/shard_map/ppermute | solution.py:391
  39.7 19.5 %collective-permute-start.27 = (bf16[64,1792]{1,0:T(8,128)(2,1)S(1)}, bf16[64,1792]{1,0:T(8,128)(2,1)S(1)}, u32[]{:S(2)}, u32[]{:S(2)}) collective-permute-start(bf16[64,1792]{1,0:T(8,128)(2,1)S(1)} %get-tuple-element.276), channel_id=1, source_target_pairs={{0,8},{1,9},{2,10},{3,11},{4,12},{5,13},{6,14},{7,15},{8,0},{9,1},... | collective-permute-start | bytes 688136 | tf_op jit(solution)/shard_map/ppermute | solution.py:391
  42.2 17.1 %collective-permute-start.28 = (bf16[64,1792]{1,0:T(8,128)(2,1)S(1)}, bf16[64,1792]{1,0:T(8,128)(2,1)S(1)}, u32[]{:S(2)}, u32[]{:S(2)}) collective-permute-start(bf16[64,1792]{1,0:T(8,128)(2,1)S(1)} %get-tuple-element.277), channel_id=1, source_target_pairs={{0,12},{1,13},{2,14},{3,15},{4,8},{5,9},{6,10},{7,11},{8,4},{9,5},... | collective-permute-start | bytes 688136 | tf_op jit(solution)/shard_map/ppermute | solution.py:391
  44.1 15.2 %collective-permute-start.29 = (bf16[64,1792]{1,0:T(8,128)(2,1)S(1)}, bf16[64,1792]{1,0:T(8,128)(2,1)S(1)}, u32[]{:S(2)}, u32[]{:S(2)}) collective-permute-start(bf16[64,1792]{1,0:T(8,128)(2,1)S(1)} %get-tuple-element.278), channel_id=1, source_target_pairs={{0,2},{1,3},{2,0},{3,1},{4,6},{5,7},{6,4},{7,5},{8,10},{9,11},{10,... | collective-permute-start | bytes 688136 | tf_op jit(solution)/shard_map/ppermute | solution.py:391
  44.7 16.5 %collective-permute-start.30 = (bf16[64,1792]{1,0:T(8,128)(2,1)S(1)}, bf16[64,1792]{1,0:T(8,128)(2,1)S(1)}, u32[]{:S(2)}, u32[]{:S(2)}) collective-permute-start(bf16[64,1792]{1,0:T(8,128)(2,1)S(1)} %get-tuple-element.279), channel_id=1, source_target_pairs={{0,6},{1,7},{2,4},{3,5},{4,2},{5,3},{6,0},{7,1},{8,14},{9,15},{10,... | collective-permute-start | bytes 688136 | tf_op jit(solution)/shard_map/ppermute | solution.py:391
  (3 other events, 8.1 us)

commit v2 on v1

--- a/solution.py
+++ b/solution.py
@@ -440,7 +440,7 @@
     def arrived(chip, plane):
         here, first, here_cross, first_cross = chip
         second, third = plane
-        return [here, swap(first, 4), swap(second, 8), swap(third, 12), swap(here_cross, 2), swap(first_cross, 6)]
+        return [here, swap(first, 4), swap(second, 8), swap(third, 12), swap(here_cross, 2), first_cross]
 
     cross_low, both_low = swap(low, 2), swap(low, 3)
     chip = jnp.concatenate([low, swap(low, 1)], axis=1)
@@ -448,7 +448,9 @@
     by_chip, cross_low, both_low = lax.optimization_barrier((by_chip, cross_low, both_low))
     plane = jnp.concatenate([chip, cross_low, both_low], axis=1)
     by_plane = plane_rows(plane[: ROOMS[0]])
-    by_plane, by_chip, x_parts = lax.optimization_barrier((by_plane, by_chip, x_parts))
+    first_cross = swap(by_chip[3], 6)
+    by_plane, by_chip, x_parts = lax.optimization_barrier((by_plane, by_chip[:3], x_parts))
+    by_chip = [*by_chip, first_cross]
     rows = arrived(by_chip, by_plane)
     gate, up = base(x_parts, gate_matrix, up_matrix, heads)
 
@@ -462,7 +464,8 @@
 
     def more(room):
         at = slice(ROOMS[0], ROOMS[0] + room)
-        rest = arrived(chip_rows(chip[at]), plane_rows(plane[at]))
+        more_chip = chip_rows(chip[at])
+        rest = arrived([*more_chip[:3], swap(more_chip[3], 6)], plane_rows(plane[at]))
         pick = jnp.concatenate([first, picked(ROOMS[0], room)], axis=1)
         return finish(gate, up, pick, order, rows + rest)
 

time: 63 us -> 62.7 us (level)
  transfers between devices with their start and end apart: 21 -> 21, of which waited for: 7 -> 7; matrix products, arithmetic and copies ran while one was open for 1% -> 1% of each run, Pallas kernels for 39% -> 40%
where the time goes in v2:
time: 62.7 us; the launch traced here: 62.4 us
  Pallas kernels  27.4 us (44%)
  starting transfers between devices  19.9 us (32%)
  waiting for transfers between devices  13.6 us (22%)
  between operations  0.92 us (1%)
    ppermute x19, starting transfers between devices, swap(): return lax.ppermute(value, 'dp', [(d, d ^ k) for d in range(count)])  16.8 us
    pallas_call x1, Pallas kernels, base(): pl.pallas_call(functools.partial(base_kernel, steps, rows), out_shape=[sh...  14.5 us
    ppermute x19, waiting for transfers between devices, swap(): return lax.ppermute(value, 'dp', [(d, d ^ k) for d in range(count)])  12.3 us
    pallas_call x2, Pallas kernels, fetch(): pl.pallas_call(functools.partial(fetch_kernel, 0), out_shape=shape, in_sp...  6.19 us
    ppermute x2, starting transfers between devices, other(): return lax.ppermute(value, 'groups', [(0, 1), (1, 0)])  3.17 us
    pallas_call x1, Pallas kernels, repack(): pl.pallas_call(functools.partial(repack_kernel, width), out_shape=[for_ro...  1.94 us
    pallas_call x1, Pallas kernels, finish(): pl.pallas_call(functools.partial(finish_kernel, width // n), out_shape=pl...  1.56 us
    ppermute x2, waiting for transfers between devices, other(): return lax.ppermute(value, 'groups', [(0, 1), (1, 0)])  1.26 us
  transfers between devices with their start and end apart: 21, of which 7 were waited for; matrix products, arithmetic and copies ran while one was open for 1% of the time, Pallas kernels for 40%

profile of v2, /device:TPU:0, one launch (start us, length us, event | category | flops | bytes accessed | tf_op | source)
XLA Modules:
  0.0 62.4 jit_solution(16677054109051922574)
XLA Ops:
  0.0 1.1 %cut_cross.1 = (bf16[32,3584]{1,0:T(8,128)(2,1)S(1)}, bf16[32,3584]{1,0:T(8,128)(2,1)S(1)}) custom-call(bf16[64,28672]{1,0:T(8,128)(2,1)} %bitcast.14), custom_call_target="tpu_custom_call" | custom-call | bytes 917504 | tf_op jit(solution)/shard_map/cut_cross/pallas_call | solution.py:103
  1.3 3.0 %collective-permute-start.10 = (bf16[8,8320]{1,0:T(8,128)(2,1)S(1)}, bf16[8,8320]{1,0:T(8,128)(2,1)S(1)}, u32[]{:S(2)}, u32[]{:S(2)}) collective-permute-start(bf16[8,8320]{1,0:T(8,128)(2,1)S(1)} %pad_maximum_fusion.6), channel_id=1, source_target_pairs={{0,2},{1,3},{2,0},{3,1},{4,6},{5,7},{6,4},{7,5},{8,10},{9,11},{10,... | collective-permute-start | bytes 399368 | tf_op jit(solution)/shard_map/ppermute | solution.py:391
  4.3 3.6 %collective-permute-start.13 = (bf16[8,8320]{1,0:T(8,128)(2,1)S(1)}, bf16[8,8320]{1,0:T(8,128)(2,1)S(1)}, u32[]{:S(2)}, u32[]{:S(2)}) collective-permute-start(bf16[8,8320]{1,0:T(8,128)(2,1)S(1)} %pad_maximum_fusion.6), channel_id=1, source_target_pairs={{0,12},{1,13},{2,14},{3,15},{4,8},{5,9},{6,10},{7,11},{8,4},{9,5},... | collective-permute-start | bytes 399368 | tf_op jit(solution)/shard_map/ppermute | solution.py:391
  8.5 1.9 %repack.1 = (bf16[64,7168]{1,0:T(8,128)(2,1)S(1)}, bf16[64,3584]{1,0:T(8,128)(2,1)S(1)}, bf16[64,7168]{1,0:T(8,128)(2,1)S(1)}, bf16[64,3584]{1,0:T(8,128)(2,1)S(1)}) custom-call(bf16[64,28672]{1,0:T(8,128)(2,1)} %bitcast.15), custom_call_target="tpu_custom_call" | custom-call | bytes 5505024 | tf_op jit(solution)/shard_map/repack/pallas_call | solution.py:133
  10.4 3.1 %fetch.2.refs_6_ = bf16[2048,1792]{1,0:T(8,128)(2,1)S(1)} custom-call(bf16[64,3584]{1,0:T(8,128)(2,1)S(1)} %get-tuple-element.235.after_ref.refs_0_, bf16[8192,1792]{1,0:T(8,128)(2,1)} %refs_4_.1), custom_call_target="tpu_custom_call" | custom-call | bytes 29360128 | tf_op jit(solution)/shard_map/fetch/pallas_call | solution.py:254
  13.6 0.6 %collective-permute-start.11 = (bf16[16,8320]{1,0:T(8,128)(2,1)S(1)}, bf16[16,8320]{1,0:T(8,128)(2,1)S(1)}, u32[]{:S(2)}, u32[]{:S(2)}) collective-permute-start(bf16[16,8320]{1,0:T(8,128)(2,1)S(1)} %pad_maximum_fusion.4), channel_id=1, source_target_pairs={{0,4},{1,5},{2,6},{3,7},{4,0},{5,1},{6,2},{7,3},{8,12},{9,13},{10,... | collective-permute-start | bytes 798728 | tf_op jit(solution)/shard_map/ppermute | solution.py:391
  14.2 4.7 %collective-permute-done.12 = bf16[8,8320]{1,0:T(8,128)(2,1)S(1)} collective-permute-done((bf16[8,8320]{1,0:T(8,128)(2,1)S(1)}, bf16[8,8320]{1,0:T(8,128)(2,1)S(1)}, u32[]{:S(2)}, u32[]{:S(2)}) %collective-permute-start.12) | collective-permute-done | bytes 133152 | tf_op jit(solution)/shard_map/ppermute | solution.py:391
  19.0 0.6 collective-permute-start.16
  19.6 1.6 %collective-permute-start.17 = (bf16[64,768]{1,0:T(8,128)(2,1)S(1)}, bf16[64,768]{1,0:T(8,128)(2,1)S(1)}, u32[]{:S(2)}, u32[]{:S(2)}) collective-permute-start(bf16[64,768]{1,0:T(8,128)(2,1)S(1)} %slice.50), channel_id=1, source_target_pairs={{0,16},{16,0},{1,17},{17,1},{2,18},{18,2},{3,19},{19,3},{4,20},{20... | collective-permute-start | bytes 294920 | tf_op jit(solution)/shard_map/ppermute | solution.py:394
  21.3 3.1 %fetch.3.refs_7_ = bf16[2048,1792]{1,0:T(8,128)(2,1)S(1)} custom-call(bf16[64,3584]{1,0:T(8,128)(2,1)S(1)} %constant_dynamic-update-slice_fusion.after_ref.refs_2_, bf16[8192,1792]{1,0:T(8,128)(2,1)} %refs_5_.1), custom_call_target="tpu_custom_call" | custom-call | bytes 29360128 | tf_op jit(solution)/shard_map/fetch/pallas_call | solution.py:254
  24.6 3.4 %collective-permute-done.16 = bf16[16,8320]{1,0:T(8,128)(2,1)S(1)} collective-permute-done((bf16[16,8320]{1,0:T(8,128)(2,1)S(1)}, bf16[16,8320]{1,0:T(8,128)(2,1)S(1)}, u32[]{:S(2)}, u32[]{:S(2)}) %collective-permute-start.16) | collective-permute-done | bytes 266272 | tf_op jit(solution)/shard_map/ppermute | solution.py:391
  28.6 1.6 %collective-permute-start.25 = (bf16[64,2816]{1,0:T(8,128)(2,1)S(1)}, bf16[64,2816]{1,0:T(8,128)(2,1)S(1)}, u32[]{:S(2)}, u32[]{:S(2)}) collective-permute-start(bf16[64,2816]{1,0:T(8,128)(2,1)S(1)} %slice.54), channel_id=1, source_target_pairs={{0,16},{16,0},{1,17},{17,1},{2,18},{18,2},{3,19},{19,3},{4,20},{20... | collective-permute-start | bytes 1081352 | tf_op jit(solution)/shard_map/ppermute | solution.py:394
  30.8 1.2 %low_rows.1 = (bf16[128,64]{1,0:T(8,128)(2,1)S(1)}, s32[2,128]{1,0:T(2,128)S(1)}, bf16[128,384]{1,0:T(8,128)(2,1)S(1)}, bf16[128,128]{1,0:T(8,128)(2,1)S(1)}, s32[1]{0:T(128)}) custom-call(bf16[32,8320]{1,0:T(8,128)(2,1)S(1)} %pad_maximum_fusion.2.refs_0_, bf16[32,8320]{1,0:T(8,128)(2,1)S(1)} %pad_maximum_fusion.3.refs_1_, ...), custom_call_target="tpu_custom_call" | custom-call | bytes 4096 | tf_op jit(solution)/shard_map/low_rows/pallas_call | solution.py:191
  33.4 1.6 %collective-permute-start.22 = (bf16[128,64]{1,0:T(8,128)(2,1)S(1)}, bf16[128,64]{1,0:T(8,128)(2,1)S(1)}, u32[]{:S(2)}, u32[]{:S(2)}) collective-permute-start(bf16[128,64]{1,0:T(8,128)(2,1)S(1)} %get-tuple-element.246), channel_id=1, source_target_pairs={{0,2},{1,3},{2,0},{3,1},{4,6},{5,7},{6,4},{7,5},{8,10},{9,11},{10,... | collective-permute-start | bytes 49160 | tf_op jit(solution)/shard_map/ppermute | solution.py:391
  35.5 1.8 %collective-permute-done.22 = bf16[128,64]{1,0:T(8,128)(2,1)S(1)} collective-permute-done((bf16[128,64]{1,0:T(8,128)(2,1)S(1)}, bf16[128,64]{1,0:T(8,128)(2,1)S(1)}, u32[]{:S(2)}, u32[]{:S(2)}) %collective-permute-start.22) | collective-permute-done | bytes 16416 | tf_op jit(solution)/shard_map/ppermute | solution.py:391
  37.8 1.3 %collective-permute-done.25.refs_4_ = bf16[64,2816]{1,0:T(8,128)(2,1)S(1)} collective-permute-done((bf16[64,2816]{1,0:T(8,128)(2,1)S(1)}, bf16[64,2816]{1,0:T(8,128)(2,1)S(1)}, u32[]{:S(2)}, u32[]{:S(2)}) %collective-permute-start.25) | collective-permute-done | bytes 360480 | tf_op jit(solution)/shard_map/ppermute | solution.py:394
  39.1 0.6 delta_rows.11
  39.7 1.4 %collective-permute-start.26 = (bf16[64,1792]{1,0:T(8,128)(2,1)S(1)}, bf16[64,1792]{1,0:T(8,128)(2,1)S(1)}, u32[]{:S(2)}, u32[]{:S(2)}) collective-permute-start(bf16[64,1792]{1,0:T(8,128)(2,1)S(1)} %get-tuple-element.273), channel_id=1, source_target_pairs={{0,4},{1,5},{2,6},{3,7},{4,0},{5,1},{6,2},{7,3},{8,12},{9,13},{10,... | collective-permute-start | bytes 688136 | tf_op jit(solution)/shard_map/ppermute | solution.py:391
  41.1 1.2 %collective-permute-start.27 = (bf16[64,1792]{1,0:T(8,128)(2,1)S(1)}, bf16[64,1792]{1,0:T(8,128)(2,1)S(1)}, u32[]{:S(2)}, u32[]{:S(2)}) collective-permute-start(bf16[64,1792]{1,0:T(8,128)(2,1)S(1)} %get-tuple-element.274), channel_id=1, source_target_pairs={{0,8},{1,9},{2,10},{3,11},{4,12},{5,13},{6,14},{7,15},{8,0},{9,1},... | collective-permute-start | bytes 688136 | tf_op jit(solution)/shard_map/ppermute | solution.py:391
  42.3 1.8 %collective-permute-start.28 = (bf16[64,1792]{1,0:T(8,128)(2,1)S(1)}, bf16[64,1792]{1,0:T(8,128)(2,1)S(1)}, u32[]{:S(2)}, u32[]{:S(2)}) collective-permute-start(bf16[64,1792]{1,0:T(8,128)(2,1)S(1)} %get-tuple-element.275), channel_id=1, source_target_pairs={{0,12},{1,13},{2,14},{3,15},{4,8},{5,9},{6,10},{7,11},{8,4},{9,5},... | collective-permute-start | bytes 688136 | tf_op jit(solution)/shard_map/ppermute | solution.py:391
  44.6 14.5 %base.1 = (f32[128,1792]{1,0:T(8,128)S(1)}, f32[128,1792]{1,0:T(8,128)S(1)}) custom-call(bf16[32,8320]{1,0:T(8,128)(2,1)S(1)} %pad_maximum_fusion.2.refs_0_, bf16[32,8320]{1,0:T(8,128)(2,1)S(1)} %pad_maximum_fusion.3.refs_1_, bf16[32,8320]{1,0:T(8,128)(2,1)S(1)} %collective-permute-done.18.refs_2_, bf16[32,8320]{1,0:T(8,128)(2,1)S(1)} %collective-permute-done.19.refs_3_, ...), custom_call_target="tpu_custom_call" | custom-call | flops 7516192768 | bytes 58720256 | tf_op jit(solution)/shard_map/base/pallas_call | solution.py:319
  59.2 1.7 %collective-permute-done.28 = bf16[64,1792]{1,0:T(8,128)(2,1)S(1)} collective-permute-done((bf16[64,1792]{1,0:T(8,128)(2,1)S(1)}, bf16[64,1792]{1,0:T(8,128)(2,1)S(1)}, u32[]{:S(2)}, u32[]{:S(2)}) %collective-permute-start.28) | collective-permute-done | bytes 229408 | tf_op jit(solution)/shard_map/ppermute | solution.py:391
  60.9 1.6 %conditional.1 = (bf16[128,1792]{1,0:T(8,128)(2,1)}) conditional(s32[]{:T(128)} %bitcast.7, (f32[128,1792]{1,0:T(8,128)S(1)}, f32[128,1792]{1,0:T(8,128)S(1)}, bf16[128,384]{1,0:T(8,128)(2,1)S(1)}, bf16[128,128]{1,0:T(8,128)(2,1)S(1)}, bf16[64,1792]{1,0:T(8,128)(2,1)S(1)}, /*index=5*/bf16[64,1792]{1,0:T(8,128)(2,1)S(1)}, ...), branch_computations={%region_0.1_spmd, %region_1.2_spmd, %region_2.3_spmd} | conditional | flops 656256 | bytes 8890576 | solution.py:472
  60.9 1.6 %finish.3 = bf16[128,1792]{1,0:T(8,128)(2,1)} custom-call(f32[128,1792]{1,0:T(8,128)S(1)} %get-tuple-element.119.gate_ref, f32[128,1792]{1,0:T(8,128)S(1)} %get-tuple-element.120.up_ref, bf16[128,384]{1,0:T(8,128)(2,1)S(1)} %get-tuple-element.121.pick_ref, bf16[128,128]{1,0:T(8,128)(2,1)S(1)} %get-tuple-element.122.order_ref, ...), custom_call_target="tpu_custom_call" | custom-call | bytes 3670016 | tf_op jit(solution)/shard_map/cond/branch_0_fun/finish/pallas_call | solution.py:358
  (56 shorter events, 4.6 us)
Async XLA Ops:
  1.3 12.3 %collective-permute-start.10 = (bf16[8,8320]{1,0:T(8,128)(2,1)S(1)}, bf16[8,8320]{1,0:T(8,128)(2,1)S(1)}, u32[]{:S(2)}, u32[]{:S(2)}) collective-permute-start(bf16[8,8320]{1,0:T(8,128)(2,1)S(1)} %pad_maximum_fusion.6), channel_id=1, source_target_pairs={{0,2},{1,3},{2,0},{3,1},{4,6},{5,7},{6,4},{7,5},{8,10},{9,11},{10,... | collective-permute-start | bytes 399368 | tf_op jit(solution)/shard_map/ppermute | solution.py:391
  4.3 10.0 %collective-permute-start.13 = (bf16[8,8320]{1,0:T(8,128)(2,1)S(1)}, bf16[8,8320]{1,0:T(8,128)(2,1)S(1)}, u32[]{:S(2)}, u32[]{:S(2)}) collective-permute-start(bf16[8,8320]{1,0:T(8,128)(2,1)S(1)} %pad_maximum_fusion.6), channel_id=1, source_target_pairs={{0,12},{1,13},{2,14},{3,15},{4,8},{5,9},{6,10},{7,11},{8,4},{9,5},... | collective-permute-start | bytes 399368 | tf_op jit(solution)/shard_map/ppermute | solution.py:391
  7.9 11.1 %collective-permute-start.12 = (bf16[8,8320]{1,0:T(8,128)(2,1)S(1)}, bf16[8,8320]{1,0:T(8,128)(2,1)S(1)}, u32[]{:S(2)}, u32[]{:S(2)}) collective-permute-start(bf16[8,8320]{1,0:T(8,128)(2,1)S(1)} %pad_maximum_fusion.6), channel_id=1, source_target_pairs={{0,8},{1,9},{2,10},{3,11},{4,12},{5,13},{6,14},{7,15},{8,0},{9,1},... | collective-permute-start | bytes 399368 | tf_op jit(solution)/shard_map/ppermute | solution.py:391
  7.9 11.1 %collective-permute-start.14 = (bf16[32,3584]{1,0:T(8,128)(2,1)S(1)}, bf16[32,3584]{1,0:T(8,128)(2,1)S(1)}, u32[]{:S(2)}, u32[]{:S(2)}) collective-permute-start(bf16[32,3584]{1,0:T(8,128)(2,1)S(1)} %get-tuple-element.236), channel_id=1, source_target_pairs={{0,2},{1,3},{2,0},{3,1},{4,6},{5,7},{6,4},{7,5},{8,10},{9,11},{10,... | collective-permute-start | bytes 688136 | tf_op jit(solution)/shard_map/ppermute | solution.py:391
  8.4 10.6 %collective-permute-start.15 = (bf16[32,3584]{1,0:T(8,128)(2,1)S(1)}, bf16[32,3584]{1,0:T(8,128)(2,1)S(1)}, u32[]{:S(2)}, u32[]{:S(2)}) collective-permute-start(bf16[32,3584]{1,0:T(8,128)(2,1)S(1)} %get-tuple-element.237), channel_id=1, source_target_pairs={{0,3},{1,2},{2,1},{3,0},{4,7},{5,6},{6,5},{7,4},{8,11},{9,10},{10,... | collective-permute-start | bytes 688136 | tf_op jit(solution)/shard_map/ppermute | solution.py:391
  13.6 10.9 %collective-permute-start.11 = (bf16[16,8320]{1,0:T(8,128)(2,1)S(1)}, bf16[16,8320]{1,0:T(8,128)(2,1)S(1)}, u32[]{:S(2)}, u32[]{:S(2)}) collective-permute-start(bf16[16,8320]{1,0:T(8,128)(2,1)S(1)} %pad_maximum_fusion.4), channel_id=1, source_target_pairs={{0,4},{1,5},{2,6},{3,7},{4,0},{5,1},{6,2},{7,3},{8,12},{9,13},{10,... | collective-permute-start | bytes 798728 | tf_op jit(solution)/shard_map/ppermute | solution.py:391
  19.0 9.0 %collective-permute-start.16 = (bf16[16,8320]{1,0:T(8,128)(2,1)S(1)}, bf16[16,8320]{1,0:T(8,128)(2,1)S(1)}, u32[]{:S(2)}, u32[]{:S(2)}) collective-permute-start(bf16[16,8320]{1,0:T(8,128)(2,1)S(1)} %pad_maximum_fusion.5), channel_id=1, source_target_pairs={{0,2},{1,3},{2,0},{3,1},{4,6},{5,7},{6,4},{7,5},{8,10},{9,11},{10,... | collective-permute-start | bytes 798728 | tf_op jit(solution)/shard_map/ppermute | solution.py:391
  19.6 8.4 %collective-permute-start.17 = (bf16[64,768]{1,0:T(8,128)(2,1)S(1)}, bf16[64,768]{1,0:T(8,128)(2,1)S(1)}, u32[]{:S(2)}, u32[]{:S(2)}) collective-permute-start(bf16[64,768]{1,0:T(8,128)(2,1)S(1)} %slice.50), channel_id=1, source_target_pairs={{0,16},{16,0},{1,17},{17,1},{2,18},{18,2},{3,19},{19,3},{4,20},{20... | collective-permute-start | bytes 294920 | tf_op jit(solution)/shard_map/ppermute | solution.py:394
  21.2 13.9 %collective-permute-start.21 = (bf16[64,7168]{1,0:T(8,128)(2,1)S(1)}, bf16[64,7168]{1,0:T(8,128)(2,1)S(1)}, u32[]{:S(2)}, u32[]{:S(2)}) collective-permute-start(bf16[64,7168]{1,0:T(8,128)(2,1)S(1)} %get-tuple-element.248), channel_id=1, source_target_pairs={{0,1},{1,0},{2,3},{3,2},{4,5},{5,4},{6,7},{7,6},{8,9},{9,8},{10,11... | collective-permute-start | bytes 2752520 | tf_op jit(solution)/shard_map/ppermute | solution.py:391
  24.5 6.2 %copy-start = (bf16[1,8192,64]{1,2,0:T(8,128)(2,1)S(1)}, bf16[1,8192,64]{1,2,0:T(8,128)(2,1)}, u32[]{:S(2)}) copy-start(bf16[1,8192,64]{1,2,0:T(8,128)(2,1)} %param.16) | copy-start | bytes 3145732
  24.6 6.2 %copy-start.1 = (s32[128,1]{1,0:T(8,128)S(1)}, s32[128,1]{1,0:T(8,128)}, u32[]{:S(2)}) copy-start(s32[128,1]{1,0:T(8,128)} %constant.35.refs_7_) | copy-start | bytes 1540
  24.6 6.2 %copy-start.2 = (s32[1,128]{1,0:T(1,128)S(1)}, s32[1,128]{1,0:T(1,128)}, u32[]{:S(2)}) copy-start(s32[1,128]{1,0:T(1,128)} %constant.34.refs_6_) | copy-start | bytes 1540
  28.0 2.2 %collective-permute-start.18 = (bf16[32,8320]{1,0:T(8,128)(2,1)S(1)}, bf16[32,8320]{1,0:T(8,128)(2,1)S(1)}, u32[]{:S(2)}, u32[]{:S(2)}) collective-permute-start(bf16[32,8320]{1,0:T(8,128)(2,1)S(1)} %pad_maximum_fusion.2.refs_0_), channel_id=1, source_target_pairs={{0,1},{1,0},{2,3},{3,2},{4,5},{5,4},{6,7},{7,6},{8,9},{9,8},{10,11... | collective-permute-start | bytes 1597448 | tf_op jit(solution)/shard_map/ppermute | solution.py:391
  28.1 2.7 %collective-permute-start.19 = (bf16[32,8320]{1,0:T(8,128)(2,1)S(1)}, bf16[32,8320]{1,0:T(8,128)(2,1)S(1)}, u32[]{:S(2)}, u32[]{:S(2)}) collective-permute-start(bf16[32,8320]{1,0:T(8,128)(2,1)S(1)} %pad_maximum_fusion.3.refs_1_), channel_id=1, source_target_pairs={{0,1},{1,0},{2,3},{3,2},{4,5},{5,4},{6,7},{7,6},{8,9},{9,8},{10,11... | collective-permute-start | bytes 1597448 | tf_op jit(solution)/shard_map/ppermute | solution.py:391
  28.6 10.5 %collective-permute-start.25 = (bf16[64,2816]{1,0:T(8,128)(2,1)S(1)}, bf16[64,2816]{1,0:T(8,128)(2,1)S(1)}, u32[]{:S(2)}, u32[]{:S(2)}) collective-permute-start(bf16[64,2816]{1,0:T(8,128)(2,1)S(1)} %slice.54), channel_id=1, source_target_pairs={{0,16},{16,0},{1,17},{17,1},{2,18},{18,2},{3,19},{19,3},{4,20},{20... | collective-permute-start | bytes 1081352 | tf_op jit(solution)/shard_map/ppermute | solution.py:394
  30.2 8.9 %collective-permute-start.24 = (bf16[64,3584]{1,0:T(8,128)(2,1)S(1)}, bf16[64,3584]{1,0:T(8,128)(2,1)S(1)}, u32[]{:S(2)}, u32[]{:S(2)}) collective-permute-start(bf16[64,3584]{1,0:T(8,128)(2,1)S(1)} %get-tuple-element.255), channel_id=1, source_target_pairs={{0,1},{1,0},{2,3},{3,2},{4,5},{5,4},{6,7},{7,6},{8,9},{9,8},{10,11... | collective-permute-start | bytes 1376264 | tf_op jit(solution)/shard_map/ppermute | solution.py:391
  32.0 1.4 %collective-permute-start.20 = (bf16[128,64]{1,0:T(8,128)(2,1)S(1)}, bf16[128,64]{1,0:T(8,128)(2,1)S(1)}, u32[]{:S(2)}, u32[]{:S(2)}) collective-permute-start(bf16[128,64]{1,0:T(8,128)(2,1)S(1)} %get-tuple-element.246), channel_id=1, source_target_pairs={{0,1},{1,0},{2,3},{3,2},{4,5},{5,4},{6,7},{7,6},{8,9},{9,8},{10,11... | collective-permute-start | bytes 49160 | tf_op jit(solution)/shard_map/ppermute | solution.py:391
  32.2 3.4 %collective-permute-start.23 = (bf16[128,64]{1,0:T(8,128)(2,1)S(1)}, bf16[128,64]{1,0:T(8,128)(2,1)S(1)}, u32[]{:S(2)}, u32[]{:S(2)}) collective-permute-start(bf16[128,64]{1,0:T(8,128)(2,1)S(1)} %get-tuple-element.246), channel_id=1, source_target_pairs={{0,3},{1,2},{2,1},{3,0},{4,7},{5,6},{6,5},{7,4},{8,11},{9,10},{10,... | collective-permute-start | bytes 49160 | tf_op jit(solution)/shard_map/ppermute | solution.py:391
  33.4 4.0 %collective-permute-start.22 = (bf16[128,64]{1,0:T(8,128)(2,1)S(1)}, bf16[128,64]{1,0:T(8,128)(2,1)S(1)}, u32[]{:S(2)}, u32[]{:S(2)}) collective-permute-start(bf16[128,64]{1,0:T(8,128)(2,1)S(1)} %get-tuple-element.246), channel_id=1, source_target_pairs={{0,2},{1,3},{2,0},{3,1},{4,6},{5,7},{6,4},{7,5},{8,10},{9,11},{10,... | collective-permute-start | bytes 49160 | tf_op jit(solution)/shard_map/ppermute | solution.py:391
  37.5 21.7 %collective-permute-start.30 = (bf16[64,1792]{1,0:T(8,128)(2,1)S(1)}, bf16[64,1792]{1,0:T(8,128)(2,1)S(1)}, u32[]{:S(2)}, u32[]{:S(2)}) collective-permute-start(bf16[64,1792]{1,0:T(8,128)(2,1)S(1)} %get-tuple-element.277), channel_id=1, source_target_pairs={{0,6},{1,7},{2,4},{3,5},{4,2},{5,3},{6,0},{7,1},{8,14},{9,15},{10,... | collective-permute-start | bytes 688136 | tf_op jit(solution)/shard_map/ppermute | solution.py:391
  39.7 19.5 %collective-permute-start.26 = (bf16[64,1792]{1,0:T(8,128)(2,1)S(1)}, bf16[64,1792]{1,0:T(8,128)(2,1)S(1)}, u32[]{:S(2)}, u32[]{:S(2)}) collective-permute-start(bf16[64,1792]{1,0:T(8,128)(2,1)S(1)} %get-tuple-element.273), channel_id=1, source_target_pairs={{0,4},{1,5},{2,6},{3,7},{4,0},{5,1},{6,2},{7,3},{8,12},{9,13},{10,... | collective-permute-start | bytes 688136 | tf_op jit(solution)/shard_map/ppermute | solution.py:391
  41.1 18.1 %collective-permute-start.27 = (bf16[64,1792]{1,0:T(8,128)(2,1)S(1)}, bf16[64,1792]{1,0:T(8,128)(2,1)S(1)}, u32[]{:S(2)}, u32[]{:S(2)}) collective-permute-start(bf16[64,1792]{1,0:T(8,128)(2,1)S(1)} %get-tuple-element.274), channel_id=1, source_target_pairs={{0,8},{1,9},{2,10},{3,11},{4,12},{5,13},{6,14},{7,15},{8,0},{9,1},... | collective-permute-start | bytes 688136 | tf_op jit(solution)/shard_map/ppermute | solution.py:391
  42.3 18.5 %collective-permute-start.28 = (bf16[64,1792]{1,0:T(8,128)(2,1)S(1)}, bf16[64,1792]{1,0:T(8,128)(2,1)S(1)}, u32[]{:S(2)}, u32[]{:S(2)}) collective-permute-start(bf16[64,1792]{1,0:T(8,128)(2,1)S(1)} %get-tuple-element.275), channel_id=1, source_target_pairs={{0,12},{1,13},{2,14},{3,15},{4,8},{5,9},{6,10},{7,11},{8,4},{9,5},... | collective-permute-start | bytes 688136 | tf_op jit(solution)/shard_map/ppermute | solution.py:391
  44.1 16.8 %collective-permute-start.29 = (bf16[64,1792]{1,0:T(8,128)(2,1)S(1)}, bf16[64,1792]{1,0:T(8,128)(2,1)S(1)}, u32[]{:S(2)}, u32[]{:S(2)}) collective-permute-start(bf16[64,1792]{1,0:T(8,128)(2,1)S(1)} %get-tuple-element.276), channel_id=1, source_target_pairs={{0,2},{1,3},{2,0},{3,1},{4,6},{5,7},{6,4},{7,5},{8,10},{9,11},{10,... | collective-permute-start | bytes 688136 | tf_op jit(solution)/shard_map/ppermute | solution.py:391
  (3 other events, 8.1 us)
